TPU v7x, 768 devices: a whole 4x8x12 slice. The times are simulated.
768 devices in a mesh: row: 32 (over z_lo, x, core), col: 24 (over y, z_hi).
Axes of the slice: x: 4, y: 8, z: 12 (z_hi: 3, z_lo: 4; z = z_hi * 4 + z_lo), core: 2. Of those that a mesh axis runs over, the one named last changes fastest.
Arguments:
- populations: float32 [19, 512, 192, 128], P(None, 'row', 'col'), may hold values from 0.02 to 0.08
- link_mask: int32 [2, 512, 192, 128], P(None, 'row', 'col'), may hold values from 0 to 511, as said below
- sphere_of_cell: int32 [512, 192, 128], P('row', 'col'), may hold values from 0 to 2047, as said below
- sphere_velocity: float32 [24, 3, 2048], P('col', None, 'row'), may hold values from -0.05 to 0.05
Outputs:
- out_pops: float32 [19, 512, 192, 128], P(None, 'row', 'col')
- sphere_force: float32 [24, 3, 2048], P('col', None, 'row')
Inputs may be any that keep to these rules, and one draw needn't show every extreme that they name: `link_mask`: any pattern of bits; a blocked link needn't match any sphere geometry. `sphere_of_cell`: for a cell at x, the id s satisfies s // 64 = (x // 16 + d) mod (32) for some d in -1, 0, 1.
All inputs are finite; a program needn't handle non-finite values.
Results may differ from a plain program's by a relative error of at most 0.0001.
Values sent between devices are 32-bit elements; how exact they have to be, the bound alone decides.
No kernel may reach another device: no remote copies, remote signals or barrier semaphores. Data moves between devices by JAX's collectives and lax.ppermute only.
A program may use at most 64 MiB of HBM per device.

v0:
```python
import jax
import jax.numpy as jnp
from jax import lax
from jax.sharding import PartitionSpec as P

STEPS = 2


lattice_dirs = (
    (0, 0, 0),
    (1, 0, 0),
    (-1, 0, 0),
    (0, 1, 0),
    (0, -1, 0),
    (0, 0, 1),
    (0, 0, -1),
    (1, 1, 0),
    (-1, -1, 0),
    (1, -1, 0),
    (-1, 1, 0),
    (1, 0, 1),
    (-1, 0, -1),
    (1, 0, -1),
    (-1, 0, 1),
    (0, 1, 1),
    (0, -1, -1),
    (0, 1, -1),
    (0, -1, 1),
)
lattice_weights = (1.0 / 3.0,) + (1.0 / 18.0,) * 6 + (1.0 / 36.0,) * 12
relax_rate = 1.25


def from_behind(x, axis, by):
    count = lax.axis_size(axis)
    return lax.ppermute(x, axis, [(i, (i + by) % count) for i in range(count)])


def extended(cells, sides, width):
    for axis, dim in sides:
        count = lax.axis_size(axis)
        head = lax.slice_in_dim(cells, 0, width, axis=dim)
        tail = lax.slice_in_dim(cells, cells.shape[dim] - width, cells.shape[dim], axis=dim)
        cells = jnp.concatenate(
            [
                lax.ppermute(tail, axis, [(i, (i + 1) % count) for i in range(count)]),
                cells,
                lax.ppermute(head, axis, [((i + 1) % count, i) for i in range(count)]),
            ],
            axis=dim,
        )
    return cells


def reverse_of(index):
    if index == 0:
        return 0
    return index + 1 if index % 2 == 1 else index - 1


def link_bit(link_mask, index):
    plane = (index - 1) // 9
    offset = (index - 1) % 9
    return jnp.bitwise_and(jnp.right_shift(link_mask[plane], offset), 1)


def project(direction, vectors):
    total = None
    for axis_n in range(3):
        if direction[axis_n] != 0:
            term = direction[axis_n] * vectors[axis_n]
            total = term if total is None else total + term
    return total


def collide(current):
    density = current[0]
    for index in range(1, 19):
        density = density + current[index]
    moment = []
    for axis_n in range(3):
        total = jnp.zeros_like(density)
        for index in range(19):
            if lattice_dirs[index][axis_n] != 0:
                total = total + lattice_dirs[index][axis_n] * current[index]
        moment.append(total / density)
    speed_sq = moment[0] * moment[0] + moment[1] * moment[1] + moment[2] * moment[2]
    relaxed = []
    for index in range(19):
        if index == 0:
            along = jnp.zeros_like(density)
        else:
            along = project(lattice_dirs[index], moment)
        equil = (
            lattice_weights[index]
            * density
            * (1.0 + 3.0 * along + 4.5 * along * along - 1.5 * speed_sq)
        )
        relaxed.append(current[index] - relax_rate * (current[index] - equil))
    return relaxed


def propagate(relaxed, padded, link_mask, z_coord, cell_u, link_force):
    width_x, width_y, height = link_mask.shape[1:]
    arrived = []
    for index in range(19):
        step_x, step_y, step_z = lattice_dirs[index]
        back = reverse_of(index)
        moved = padded[index, 1 - step_x : 1 - step_x + width_x, 1 - step_y : 1 - step_y + width_y]
        if step_z != 0:
            moved = jnp.roll(moved, step_z, axis=2)
            source_z = z_coord - step_z
            moved = jnp.where((source_z < 0) | (source_z >= height), relaxed[back], moved)
        if index > 0:
            along = project(lattice_dirs[index], cell_u)
            blocked = link_bit(link_mask, back) == 1
            moved = jnp.where(blocked, relaxed[back] + 6.0 * lattice_weights[index] * along, moved)
            hit = link_bit(link_mask, index).astype(jnp.float32)
            transfer = hit * (2.0 * relaxed[index] - 6.0 * lattice_weights[index] * along)
            for axis_n in range(3):
                if lattice_dirs[index][axis_n] != 0:
                    link_force[axis_n] = link_force[axis_n] + lattice_dirs[index][axis_n] * transfer
        arrived.append(moved)
    return (arrived, link_force)


def on_device(populations, link_mask, sphere_of_cell, sphere_velocity):
    per_tile = sphere_velocity.shape[2]
    nearby = []
    for shift_by in (1, -1):
        nearby.append(from_behind(sphere_velocity, "row", shift_by))
    records = jnp.concatenate([nearby[0], sphere_velocity, nearby[1]], axis=2)
    tile_block = jnp.mod(
        sphere_of_cell // per_tile - lax.axis_index("row") + 1, lax.axis_size("row")
    )
    cell_slot = tile_block * per_tile + jnp.mod(sphere_of_cell, per_tile)
    cell_u = [records[0, axis_n][cell_slot] for axis_n in range(3)]
    height = sphere_of_cell.shape[2]
    z_coord = lax.broadcasted_iota(jnp.int32, (1, 1, height), 2)
    link_force = [jnp.zeros(sphere_of_cell.shape, jnp.float32) for axis_n in range(3)]
    current = [populations[index] for index in range(19)]
    for repeat in range(STEPS):
        relaxed = collide(current)
        stacked = jnp.stack(relaxed)
        padded = extended(stacked, (("row", 1), ("col", 2)), 1)
        current, link_force = propagate(relaxed, padded, link_mask, z_coord, cell_u, link_force)
    slot_flat = cell_slot.ravel()
    force_rows = jnp.stack([plane.ravel() for plane in link_force], axis=1)
    summed = jax.ops.segment_sum(force_rows, slot_flat, num_segments=records.shape[2])
    terms = jnp.transpose(summed)[None]
    totals = terms[:, :, per_tile : 2 * per_tile]
    for shift_by, place in ((-1, 0), (1, 2)):
        totals = totals + from_behind(
            terms[:, :, place * per_tile : (place + 1) * per_tile], "row", shift_by
        )
    return (jnp.stack(current), totals)


def solution(mesh):
    in_specs = (
        P(None, "row", "col", None),
        P(None, "row", "col", None),
        P("row", "col", None),
        P("col", None, "row"),
    )
    out_specs = (P(None, "row", "col", None), P("col", None, "row"))
    return jax.shard_map(
        on_device, mesh=mesh, in_specs=in_specs, out_specs=out_specs, check_vma=False
    )
```

profile of v0, /device:TPU:56, one launch (start us, length us, event | category | flops | bytes accessed | tf_op | source)
XLA Modules:
  0.0 631.5 jit_solution(8453368051419290347)
XLA Ops:
  0.6 2.1 collective-permute-start
  2.7 9.5 %collective-permute-start.1 = (f32[1,3,64]{2,0,1:T(1,128)}, f32[1,3,64]{2,0,1:T(1,128)S(1)}, u32[]{:S(2)}, u32[]{:S(2)}) collective-permute-start(f32[1,3,64]{2,0,1:T(1,128)} %param.7), channel_id=1, source_target_pairs={{0,744},{24,0},{48,24},{72,48},{96,72},{120,96},{144,120},{168,144... | collective-permute-start | bytes 2312 | tf_op jit(solution)/shard_map/ppermute | solution.py:36
  12.2 2.1 constant_dynamic-update-slice_fusion.18
  20.9 1.0 constant_dynamic-update-slice_fusion.7
  26.7 2.6 collective-permute-start.3
  29.3 1.9 collective-permute-start.2
  31.3 1.1 fusion.463
  34.5 101.4 %gather_fusion.2 = f32[16384]{0:T(1024)S(1)} fusion(f32[192]{0:T(256)S(1)} %bitcast.1118, s32[16384]{0:T(1024)S(1)} %get-tuple-element.130), kind=kCustom, calls=%fused_computation.2 | custom fusion | bytes 196608 | tf_op jit(solution)/shard_map/gather | solution.py:137
  135.9 101.4 %gather_fusion.1 = f32[16384]{0:T(1024)S(1)} fusion(f32[192]{0:T(256)S(1)} %bitcast.1117, s32[16384]{0:T(1024)S(1)} %get-tuple-element.130), kind=kCustom, calls=%fused_computation.1 | custom fusion | bytes 196608 | tf_op jit(solution)/shard_map/gather | solution.py:137
  237.3 101.4 %gather_fusion = f32[16384]{0:T(1024)S(1)} fusion(f32[192]{0:T(256)S(1)} %bitcast.1116, s32[16384]{0:T(1024)S(1)} %get-tuple-element.130), kind=kCustom, calls=%fused_computation | custom fusion | bytes 196608 | tf_op jit(solution)/shard_map/gather | solution.py:137
  344.3 13.2 %collective-permute-start.5 = (f32[19,18,1,128]{3,2,1,0:T(1,128)S(1)}, f32[19,18,1,128]{3,2,1,0:T(1,128)S(1)}, u32[]{:S(2)}, u32[]{:S(2)}) collective-permute-start(f32[19,18,1,128]{3,2,1,0:T(1,128)S(1)} %get-tuple-element.218), channel_id=1, source_target_pairs={{1,0},{2,1},{3,2},{4,3},{5,4},{6,5},{7,6},{8,7},{9,8},{10,9},{11,1... | collective-permute-start | bytes 525320 | tf_op jit(solution)/shard_map/ppermute | solution.py:48
  357.5 2.1 collective-permute-start.4
  360.4 0.9 fusion.394
  361.3 7.9 %collective-permute-done.5 = f32[19,18,1,128]{3,2,1,0:T(1,128)S(1)} collective-permute-done((f32[19,18,1,128]{3,2,1,0:T(1,128)S(1)}, f32[19,18,1,128]{3,2,1,0:T(1,128)S(1)}, u32[]{:S(2)}, u32[]{:S(2)}) %collective-permute-start.5) | collective-permute-done | bytes 175136 | tf_op jit(solution)/shard_map/ppermute | solution.py:48
  369.2 9.8 %collective-permute-done.4 = f32[19,18,1,128]{3,2,1,0:T(1,128)S(1)} collective-permute-done((f32[19,18,1,128]{3,2,1,0:T(1,128)S(1)}, f32[19,18,1,128]{3,2,1,0:T(1,128)S(1)}, u32[]{:S(2)}, u32[]{:S(2)}) %collective-permute-start.4) | collective-permute-done | bytes 175136 | tf_op jit(solution)/shard_map/ppermute | solution.py:46
  381.1 1.5 copy.40
  382.6 1.5 slice.563
  384.2 1.5 copy.46
  385.7 1.6 slice_bitcast_fusion.10
  387.3 1.6 slice_bitcast_fusion.12
  389.0 1.7 fusion.385
  392.2 1.9 select_select_fusion.1
  395.4 1.5 copy.44
  397.0 1.5 copy.42
  398.5 1.4 copy.43
  399.9 1.4 copy.45
  401.4 1.4 copy.41
  402.8 1.4 copy.47
  404.2 1.4 copy.31
  405.6 1.5 copy.28
  407.2 1.4 copy.29
  408.6 1.1 select_select_fusion
  412.0 2.4 multiply_subtract_fusion.18
  415.4 1.7 constant_dynamic-update-slice_fusion.56
  430.5 15.9 %multiply_add_fusion = f32[16384,1]{0,1:T(1,128)S(1)} fusion(f32[16384,1]{0,1:T(1,128)} %bitcast.1338, f32[16384,1]{0,1:T(1,128)} %bitcast.1339, f32[16384,1]{0,1:T(1,128)S(1)} %bitcast.1125, f32[16384,1]{0,1:T(1,128)S(1)} %bitcast.1299, f32[16384,1]{0,1:T(1,128)S(1)} %bitcast.1315, f32[16384,1]{0,1:T(1,128)S(1)} %bitcast.1301, ...), kind=kLoop, calls=%fused_computation.799 | loop fusion | flops 10092544 | bytes 3670016 | tf_op jit(solution)/shard_map/add | solution.py:122
  446.5 15.1 %add_add_fusion = f32[16384,1]{0,1:T(1,128)S(1)} fusion(f32[16384,1]{0,1:T(1,128)} %bitcast.1336, f32[16384,1]{0,1:T(1,128)} %bitcast.1337, f32[16384,1]{0,1:T(1,128)S(1)} %bitcast.1120, f32[16384,1]{0,1:T(1,128)S(1)} %bitcast.1307, f32[16384,1]{0,1:T(1,128)S(1)} %bitcast.1316, f32[16384,1]{0,1:T(1,128)S(1)} %bitcast.1311, f32[16384,1]{0,1:T(1,128)S(1)} %bitcast.1309, ...), kind=kLoop, calls=%fused_computation.798 | loop fusion | flops 10092544 | bytes 3670016 | tf_op jit(solution)/shard_map/add | solution.py:122
  461.6 15.6 %multiply_add_fusion.1 = f32[16384,1]{0,1:T(1,128)S(1)} fusion(f32[16384,1]{0,1:T(1,128)S(1)} %bitcast.1335, f32[16384,1]{0,1:T(1,128)S(1)} %bitcast.1334, f32[16384,1]{0,1:T(1,128)S(1)} %bitcast.1124, f32[16384,1]{0,1:T(1,128)S(1)} %bitcast.1300, f32[16384,1]{0,1:T(1,128)S(1)} %bitcast.1308, f32[16384,1]{0,1:T(1,128)S(1)} %bitcast.1302, ...), kind=kLoop, calls=%fused_computation.808 | loop fusion | flops 10092544 | bytes 3670016 | tf_op jit(solution)/shard_map/add | solution.py:122
  477.4 5.1 copy.68
  482.5 87.6 %scatter_custom_fusion = f32[192,3]{1,0:T(8,128)S(1)} fusion(s32[16384]{0:T(1024)} %bitcast.1340, f32[16384,3]{1,0:T(8,128)} %copy.68, f32[]{:T(128)} %constant.109.clone.1), kind=kCustom, calls=%fused_computation.957 | custom fusion | flops 49152 | bytes 2816 | tf_op jit(solution)/shard_map/scatter-add | solution.py:149
  570.7 5.8 collective-permute-start.10
  576.5 1.9 collective-permute-start.11
  580.4 7.5 %collective-permute-start.7 = (f32[19,1,8,128]{3,2,1,0:T(8,128)}, f32[19,1,8,128]{3,2,1,0:T(8,128)S(1)}, u32[]{:S(2)}, u32[]{:S(2)}) collective-permute-start(f32[19,1,8,128]{3,2,1,0:T(8,128)} %get-tuple-element.248), channel_id=1, source_target_pairs={{24,0},{48,24},{72,48},{96,72},{120,96},{144,120},{168,144},{192,1... | collective-permute-start | bytes 233480 | tf_op jit(solution)/shard_map/ppermute | solution.py:48
  587.9 1.9 collective-permute-start.6
  590.5 16.2 %collective-permute-done.6 = f32[19,1,8,128]{3,2,1,0:T(8,128)S(1)} collective-permute-done((f32[19,1,8,128]{3,2,1,0:T(8,128)}, f32[19,1,8,128]{3,2,1,0:T(8,128)S(1)}, u32[]{:S(2)}, u32[]{:S(2)}) %collective-permute-start.6) | collective-permute-done | bytes 77856 | tf_op jit(solution)/shard_map/ppermute | solution.py:46
  606.9 4.7 collective-permute-start.9
  611.6 5.1 collective-permute-start.8
  616.8 7.0 %collective-permute-done.8 = f32[19,18,1,128]{3,2,1,0:T(1,128)S(1)} collective-permute-done((f32[19,18,1,128]{3,2,1,0:T(1,128)S(1)}, f32[19,18,1,128]{3,2,1,0:T(1,128)S(1)}, u32[]{:S(2)}, u32[]{:S(2)}) %collective-permute-start.8) | collective-permute-done | bytes 175136 | tf_op jit(solution)/shard_map/ppermute | solution.py:46
  630.5 1.0 copy-done.6
  (398 shorter events, 50.4 us)
Async XLA Ops:
  0.6 13.7 %copy-start = (f32[19,16,8,128]{3,2,1,0:T(8,128)S(1)}, f32[19,16,8,128]{3,2,1,0:T(8,128)}, u32[]{:S(2)}) copy-start(f32[19,16,8,128]{3,2,1,0:T(8,128)} %param.4) | copy-start | bytes 3735556
  0.6 33.8 %collective-permute-start = (f32[1,3,64]{2,0,1:T(1,128)}, f32[1,3,64]{2,0,1:T(1,128)S(1)}, u32[]{:S(2)}, u32[]{:S(2)}) collective-permute-start(f32[1,3,64]{2,0,1:T(1,128)} %param.7), channel_id=1, source_target_pairs={{0,24},{24,48},{48,72},{72,96},{96,120},{120,144},{144,168},{168,1... | collective-permute-start | bytes 2312 | tf_op jit(solution)/shard_map/ppermute | solution.py:36
  2.7 31.7 %collective-permute-start.1 = (f32[1,3,64]{2,0,1:T(1,128)}, f32[1,3,64]{2,0,1:T(1,128)S(1)}, u32[]{:S(2)}, u32[]{:S(2)}) collective-permute-start(f32[1,3,64]{2,0,1:T(1,128)} %param.7), channel_id=1, source_target_pairs={{0,744},{24,0},{48,24},{72,48},{96,72},{120,96},{144,120},{168,144... | collective-permute-start | bytes 2312 | tf_op jit(solution)/shard_map/ppermute | solution.py:36
  23.4 7.8 %copy-start.1 = (s32[2,16,8,128]{3,2,1,0:T(8,128)S(1)}, s32[2,16,8,128]{3,2,1,0:T(8,128)}, u32[]{:S(2)}) copy-start(s32[2,16,8,128]{3,2,1,0:T(8,128)} %param.5) | copy-start | bytes 393220
  25.4 6.9 %copy-start.129 = (s32[16,8,128]{2,1,0:T(8,128)S(1)}, s32[16,8,128]{2,1,0:T(8,128)}, u32[]{:S(2)}) copy-start(s32[16,8,128]{2,1,0:T(8,128)} %param.6) | copy-start | bytes 196612
  26.0 8.4 %copy-start.130 = (f32[1,3,64]{2,0,1:T(1,128)S(1)}, f32[1,3,64]{2,0,1:T(1,128)}, u32[]{:S(2)}) copy-start(f32[1,3,64]{2,0,1:T(1,128)} %param.7) | copy-start | bytes 2308
  26.7 312.0 %collective-permute-start.3 = (f32[19,1,8,128]{3,2,1,0:T(8,128)S(1)}, f32[19,1,8,128]{3,2,1,0:T(8,128)S(1)}, u32[]{:S(2)}, u32[]{:S(2)}) collective-permute-start(f32[19,1,8,128]{3,2,1,0:T(8,128)S(1)} %get-tuple-element.252), channel_id=1, source_target_pairs={{24,0},{48,24},{72,48},{96,72},{120,96},{144,120},{168,144},{192,1... | collective-permute-start | bytes 233480 | tf_op jit(solution)/shard_map/ppermute | solution.py:48
  29.3 309.4 %collective-permute-start.2 = (f32[19,1,8,128]{3,2,1,0:T(8,128)S(1)}, f32[19,1,8,128]{3,2,1,0:T(8,128)S(1)}, u32[]{:S(2)}, u32[]{:S(2)}) collective-permute-start(f32[19,1,8,128]{3,2,1,0:T(8,128)S(1)} %get-tuple-element.253), channel_id=1, source_target_pairs={{0,24},{24,48},{48,72},{72,96},{96,120},{120,144},{144,168},{168,1... | collective-permute-start | bytes 233480 | tf_op jit(solution)/shard_map/ppermute | solution.py:46
  338.8 5.5 copy-start.35
  338.8 5.5 copy-start.36
  339.8 4.5 copy-start.68
  344.3 25.0 %collective-permute-start.5 = (f32[19,18,1,128]{3,2,1,0:T(1,128)S(1)}, f32[19,18,1,128]{3,2,1,0:T(1,128)S(1)}, u32[]{:S(2)}, u32[]{:S(2)}) collective-permute-start(f32[19,18,1,128]{3,2,1,0:T(1,128)S(1)} %get-tuple-element.218), channel_id=1, source_target_pairs={{1,0},{2,1},{3,2},{4,3},{5,4},{6,5},{7,6},{8,7},{9,8},{10,9},{11,1... | collective-permute-start | bytes 525320 | tf_op jit(solution)/shard_map/ppermute | solution.py:48
  357.5 21.5 %collective-permute-start.4 = (f32[19,18,1,128]{3,2,1,0:T(1,128)S(1)}, f32[19,18,1,128]{3,2,1,0:T(1,128)S(1)}, u32[]{:S(2)}, u32[]{:S(2)}) collective-permute-start(f32[19,18,1,128]{3,2,1,0:T(1,128)S(1)} %get-tuple-element.219), channel_id=1, source_target_pairs={{0,1},{1,2},{2,3},{3,4},{4,5},{5,6},{6,7},{7,8},{8,9},{9,10},{10,1... | collective-permute-start | bytes 525320 | tf_op jit(solution)/shard_map/ppermute | solution.py:46
  369.2 9.8 %copy-start.2 = (f32[19,18,1,128]{3,2,1,0:T(1,128)}, f32[19,18,1,128]{3,2,1,0:T(1,128)S(1)}, u32[]{:S(2)}) copy-start(f32[19,18,1,128]{3,2,1,0:T(1,128)S(1)} %collective-permute-done.5) | copy-start | bytes 525316
  379.8 9.2 %copy-start.37 = (f32[16,8,128]{2,1,0:T(8,128)}, f32[16,8,128]{2,1,0:T(8,128)S(1)}, u32[]{:S(2)}) copy-start(f32[16,8,128]{2,1,0:T(8,128)S(1)} %get-tuple-element.210) | copy-start | bytes 196612
  409.7 51.8 %copy-start.42 = (pred[1,16,8,128]{3,2,1,0:T(8,128)(4,1)}, pred[1,16,8,128]{3,2,1,0:T(8,128)(4,1)S(1)}, u32[]{:S(2)}) copy-start(pred[1,16,8,128]{3,2,1,0:T(8,128)(4,1)S(1)} %get-tuple-element.195) | copy-start | bytes 49156
  409.7 51.8 %copy-start.45 = (pred[1,16,8,128]{3,2,1,0:T(8,128)(4,1)}, pred[1,16,8,128]{3,2,1,0:T(8,128)(4,1)S(1)}, u32[]{:S(2)}) copy-start(pred[1,16,8,128]{3,2,1,0:T(8,128)(4,1)S(1)} %get-tuple-element.63) | copy-start | bytes 49156
  410.7 50.9 %copy-start.60 = (pred[1,16,8,128]{3,2,1,0:T(8,128)(4,1)}, pred[1,16,8,128]{3,2,1,0:T(8,128)(4,1)S(1)}, u32[]{:S(2)}) copy-start(pred[1,16,8,128]{3,2,1,0:T(8,128)(4,1)S(1)} %get-tuple-element.180) | copy-start | bytes 49156
  410.7 50.9 %copy-start.62 = (pred[1,16,8,128]{3,2,1,0:T(8,128)(4,1)}, pred[1,16,8,128]{3,2,1,0:T(8,128)(4,1)S(1)}, u32[]{:S(2)}) copy-start(pred[1,16,8,128]{3,2,1,0:T(8,128)(4,1)S(1)} %get-tuple-element.36) | copy-start | bytes 49156
  426.5 3.7 copy-start.11
  426.5 3.7 copy-start.12
  426.5 3.7 copy-start.13
  426.6 3.7 copy-start.14
  426.6 3.7 copy-start.15
  426.6 3.7 copy-start.16
  426.6 3.7 copy-start.17
  426.6 3.7 copy-start.18
  426.6 3.7 copy-start.19
  426.6 3.7 copy-start.20
  426.6 3.7 copy-start.21
  430.5 15.9 %copy-start.52 = (f32[1,16,8,128]{3,2,1,0:T(8,128)S(1)}, f32[1,16,8,128]{3,2,1,0:T(8,128)}, u32[]{:S(2)}) copy-start(f32[1,16,8,128]{3,2,1,0:T(8,128)} %get-tuple-element.264) | copy-start | bytes 196612
  430.5 15.9 %copy-start.53 = (f32[1,16,8,128]{3,2,1,0:T(8,128)S(1)}, f32[1,16,8,128]{3,2,1,0:T(8,128)}, u32[]{:S(2)}) copy-start(f32[1,16,8,128]{3,2,1,0:T(8,128)} %get-tuple-element.265) | copy-start | bytes 196612
  430.5 15.9 %copy-start.54 = (f32[1,16,8,128]{3,2,1,0:T(8,128)S(1)}, f32[1,16,8,128]{3,2,1,0:T(8,128)}, u32[]{:S(2)}) copy-start(f32[1,16,8,128]{3,2,1,0:T(8,128)} %get-tuple-element.266) | copy-start | bytes 196612
  430.5 15.9 %copy-start.55 = (f32[1,16,8,128]{3,2,1,0:T(8,128)S(1)}, f32[1,16,8,128]{3,2,1,0:T(8,128)}, u32[]{:S(2)}) copy-start(f32[1,16,8,128]{3,2,1,0:T(8,128)} %get-tuple-element.267) | copy-start | bytes 196612
  446.5 15.1 %copy-start.71 = (f32[1,16,8,128]{3,2,1,0:T(8,128)S(1)}, f32[1,16,8,128]{3,2,1,0:T(8,128)}, u32[]{:S(2)}) copy-start(f32[1,16,8,128]{3,2,1,0:T(8,128)} %get-tuple-element.254) | copy-start | bytes 196612
  446.5 15.1 %copy-start.72 = (f32[1,16,8,128]{3,2,1,0:T(8,128)S(1)}, f32[1,16,8,128]{3,2,1,0:T(8,128)}, u32[]{:S(2)}) copy-start(f32[1,16,8,128]{3,2,1,0:T(8,128)} %get-tuple-element.255) | copy-start | bytes 196612
  477.3 101.0 %copy-start.64 = (f32[16,8,128]{2,1,0:T(8,128)S(1)}, f32[16,8,128]{2,1,0:T(8,128)}, u32[]{:S(2)}) copy-start(f32[16,8,128]{2,1,0:T(8,128)} %get-tuple-element.6) | copy-start | bytes 196612
  477.4 101.1 %copy-start.66 = (f32[16,8,128]{2,1,0:T(8,128)S(1)}, f32[16,8,128]{2,1,0:T(8,128)}, u32[]{:S(2)}) copy-start(f32[16,8,128]{2,1,0:T(8,128)} %copy-done.65) | copy-start | bytes 196612
  570.7 46.0 %copy-start.119 = (f32[1,16,8,128]{3,2,1,0:T(8,128)S(1)}, f32[1,16,8,128]{3,2,1,0:T(8,128)}, u32[]{:S(2)}) copy-start(f32[1,16,8,128]{3,2,1,0:T(8,128)} %get-tuple-element.103) | copy-start | bytes 196612
  570.7 19.1 %collective-permute-start.10 = (f32[1,3,64]{1,2,0:T(8,128)}, f32[1,3,64]{1,2,0:T(8,128)S(1)}, u32[]{:S(2)}, u32[]{:S(2)}) collective-permute-start(f32[1,3,64]{1,2,0:T(8,128)} %get-tuple-element.272), channel_id=1, source_target_pairs={{0,744},{24,0},{48,24},{72,48},{96,72},{120,96},{144,120},{168,144... | collective-permute-start | bytes 2312 | tf_op jit(solution)/shard_map/ppermute | solution.py:36
  576.5 13.4 %collective-permute-start.11 = (f32[1,3,64]{1,2,0:T(8,128)S(1)}, f32[1,3,64]{1,2,0:T(8,128)S(1)}, u32[]{:S(2)}, u32[]{:S(2)}) collective-permute-start(f32[1,3,64]{1,2,0:T(8,128)S(1)} %get-tuple-element.273), channel_id=1, source_target_pairs={{0,24},{24,48},{48,72},{72,96},{96,120},{120,144},{144,168},{168,1... | collective-permute-start | bytes 2312 | tf_op jit(solution)/shard_map/ppermute | solution.py:36
  580.4 10.2 %collective-permute-start.7 = (f32[19,1,8,128]{3,2,1,0:T(8,128)}, f32[19,1,8,128]{3,2,1,0:T(8,128)S(1)}, u32[]{:S(2)}, u32[]{:S(2)}) collective-permute-start(f32[19,1,8,128]{3,2,1,0:T(8,128)} %get-tuple-element.248), channel_id=1, source_target_pairs={{24,0},{48,24},{72,48},{96,72},{120,96},{144,120},{168,144},{192,1... | collective-permute-start | bytes 233480 | tf_op jit(solution)/shard_map/ppermute | solution.py:48
  587.9 18.8 %collective-permute-start.6 = (f32[19,1,8,128]{3,2,1,0:T(8,128)}, f32[19,1,8,128]{3,2,1,0:T(8,128)S(1)}, u32[]{:S(2)}, u32[]{:S(2)}) collective-permute-start(f32[19,1,8,128]{3,2,1,0:T(8,128)} %get-tuple-element.249), channel_id=1, source_target_pairs={{0,24},{24,48},{48,72},{72,96},{96,120},{120,144},{144,168},{168,1... | collective-permute-start | bytes 233480 | tf_op jit(solution)/shard_map/ppermute | solution.py:46
  590.5 26.2 %copy-start.118 = (f32[1,16,8,128]{3,2,1,0:T(8,128)S(1)}, f32[1,16,8,128]{3,2,1,0:T(8,128)}, u32[]{:S(2)}) copy-start(f32[1,16,8,128]{3,2,1,0:T(8,128)} %get-tuple-element.105) | copy-start | bytes 196612
  606.9 16.9 %collective-permute-start.9 = (f32[19,18,1,128]{3,2,1,0:T(1,128)S(1)}, f32[19,18,1,128]{3,2,1,0:T(1,128)S(1)}, u32[]{:S(2)}, u32[]{:S(2)}) collective-permute-start(f32[19,18,1,128]{3,2,1,0:T(1,128)S(1)} %get-tuple-element.214), channel_id=1, source_target_pairs={{1,0},{2,1},{3,2},{4,3},{5,4},{6,5},{7,6},{8,7},{9,8},{10,9},{11,1... | collective-permute-start | bytes 525320 | tf_op jit(solution)/shard_map/ppermute | solution.py:48
  611.6 12.1 %collective-permute-start.8 = (f32[19,18,1,128]{3,2,1,0:T(1,128)S(1)}, f32[19,18,1,128]{3,2,1,0:T(1,128)S(1)}, u32[]{:S(2)}, u32[]{:S(2)}) collective-permute-start(f32[19,18,1,128]{3,2,1,0:T(1,128)S(1)} %get-tuple-element.215), channel_id=1, source_target_pairs={{0,1},{1,2},{2,3},{3,4},{4,5},{5,6},{6,7},{7,8},{8,9},{9,10},{10,1... | collective-permute-start | bytes 525320 | tf_op jit(solution)/shard_map/ppermute | solution.py:46
  616.7 7.1 %copy-start.128 = (f32[1,16,8,128]{3,2,1,0:T(8,128)S(1)}, f32[1,16,8,128]{3,2,1,0:T(8,128)}, u32[]{:S(2)}) copy-start(f32[1,16,8,128]{3,2,1,0:T(8,128)} %get-tuple-element.99) | copy-start | bytes 196612
  616.8 7.1 %copy-start.127 = (f32[1,16,8,128]{3,2,1,0:T(8,128)S(1)}, f32[1,16,8,128]{3,2,1,0:T(8,128)}, u32[]{:S(2)}) copy-start(f32[1,16,8,128]{3,2,1,0:T(8,128)} %get-tuple-element.101) | copy-start | bytes 196612
  (95 other events, 270.0 us)
where the time goes:
time: 633 us; the launch traced here: 631 us
  local copies, waits for them, and re-layouts  354 us (56%)
  other arithmetic  176 us (28%)
  starting transfers between devices  58.2 us (9%)
  waiting for transfers between devices  40.9 us (6%)
    gather x3, local copies, waits for them, and re-layouts, on_device(): cell_u = [records[0, axis_n][cell_slot] for axis_n in range(3)]  304 us
    scatter-add x1, other arithmetic, on_device(): jax.ops.segment_sum(force_rows, slot_flat, num_segments=records.shape[2])  87.6 us
    add x3, other arithmetic, propagate(): link_force[axis_n] + lattice_dirs[index][axis_n] * transfer  46.5 us
    ppermute x4, waiting for transfers between devices, extended(): lax.ppermute(tail, axis, [(i, (i + 1) % count) for i in range(count)])  32.9 us
    ppermute x4, starting transfers between devices, extended(): lax.ppermute(head, axis, [((i + 1) % count, i) for i in range(count)])  28 us
    unnamed x50, other arithmetic  27.7 us
    concatenate x36, local copies, waits for them, and re-layouts, propagate(): moved = jnp.roll(moved, step_z, axis=2)  21.4 us
    ppermute x4, starting transfers between devices, from_behind(): return lax.ppermute(x, axis, [(i, (i + by) % count) for i in range(count)])  19.3 us
  transfers between devices with their start and end apart: 12, of which 4 were waited for; matrix products, arithmetic and copies ran while one was open for 52% of the time, Pallas kernels for 0%

commit v1 on v0

v1 whole, which is shorter than its diff:
```python
import functools

import jax
import jax.numpy as jnp
from jax import lax
from jax.experimental import pallas as pl
from jax.experimental.pallas import tpu as pltpu
from jax.sharding import PartitionSpec as P

DIRS = (
    (0, 0, 0),
    (1, 0, 0),
    (-1, 0, 0),
    (0, 1, 0),
    (0, -1, 0),
    (0, 0, 1),
    (0, 0, -1),
    (1, 1, 0),
    (-1, -1, 0),
    (1, -1, 0),
    (-1, 1, 0),
    (1, 0, 1),
    (-1, 0, -1),
    (1, 0, -1),
    (-1, 0, 1),
    (0, 1, 1),
    (0, -1, -1),
    (0, 1, -1),
    (0, -1, 1),
)
WEIGHTS = (1.0 / 3.0,) + (1.0 / 18.0,) * 6 + (1.0 / 36.0,) * 12
RELAX = 1.25
F32 = jnp.float32
CX, CY, NZ, PER = 16, 8, 128, 64
ROWS = CX * CY
XP = tuple(i for i in range(19) if DIRS[i][0] == 1)
XM = tuple(i for i in range(19) if DIRS[i][0] == -1)
YP = tuple(i for i in range(19) if DIRS[i][1] == 1)
YM = tuple(i for i in range(19) if DIRS[i][1] == -1)
YMSG = 264
VMEM_LIMIT = 40 * 1024 * 1024


def opp(i):
    return 0 if i == 0 else (i + 1 if i % 2 == 1 else i - 1)


def project(direction, vec):
    total = None
    for k in range(3):
        if direction[k] != 0:
            term = vec[k] if direction[k] == 1 else -vec[k]
            total = term if total is None else total + term
    return total


def bit_set(masks, j):
    return jnp.bitwise_and(masks[(j - 1) // 9], 1 << ((j - 1) % 9)) != 0


def wall_terms(vel):
    terms = [None] * 19
    for i in range(1, 19, 2):
        along = (6.0 * WEIGHTS[i]) * project(DIRS[i], vel)
        terms[i] = along
        terms[i + 1] = -along
    return terms


def moments(f):
    rho = f[0]
    for i in range(1, 19):
        rho = rho + f[i]
    mom = []
    for k in range(3):
        total = None
        for i in range(19):
            if DIRS[i][k] != 0:
                if total is None:
                    total = f[i]
                elif DIRS[i][k] == 1:
                    total = total + f[i]
                else:
                    total = total - f[i]
        mom.append(total)
    return rho, mom


def relaxed(f, which, rho, mom):
    inv = 1.0 / rho
    u = [m * inv for m in mom]
    base = 1.0 - 1.5 * (u[0] * u[0] + u[1] * u[1] + u[2] * u[2])
    out = {}
    scaled = {w: (RELAX * w) * rho for w in sorted({WEIGHTS[i] for i in which})}
    for i in which:
        if i == 0:
            shape = base
        else:
            along = project(DIRS[i], u)
            shape = base + along * (3.0 + 4.5 * along)
        out[i] = (1.0 - RELAX) * f[i] + scaled[WEIGHTS[i]] * shape
    return out


def iota(shape, dim):
    return lax.broadcasted_iota(jnp.int32, shape, dim)


def roll(x, by, axis):
    return pltpu.roll(x, by % x.shape[axis], axis)


def slots(ids):
    count = lax.axis_size("row")
    block = jnp.right_shift(ids, 6) - lax.axis_index("row") + 1
    block = jnp.where(block < 0, block + count, block)
    block = jnp.where(block >= count, block - count, block)
    return block, jnp.bitwise_and(ids, PER - 1)


def tables(left, own, right, shape):
    low = iota((8, NZ), 1) < PER
    pair = jnp.where(low, left, roll(own, PER, 1))
    near = [jnp.broadcast_to(pair[k : k + 1], shape) for k in range(3)]
    far = [jnp.broadcast_to(right[k : k + 1], shape) for k in range(3)]
    return near, far


def velocity_of(ids, near, far):
    block, member = slots(ids)
    index = jnp.where(block == 1, member + PER, member)
    is_far = block == 2
    out = []
    for k in range(3):
        a = jnp.take_along_axis(near[k], index, axis=1, mode="promise_in_bounds")
        b = jnp.take_along_axis(far[k], index, axis=1, mode="promise_in_bounds")
        out.append(jnp.where(is_far, b, a))
    return out


def z_edge(shape, step):
    return iota(shape, 1) == (0 if step == 1 else NZ - 1)


def plane_at(ref, i, x):
    start = x * CY if isinstance(x, int) else pl.multiple_of(x * CY, CY)
    return ref[i, pl.ds(start, CY), :]


def put_plane(ref, i, x, value):
    start = x * CY if isinstance(x, int) else pl.multiple_of(x * CY, CY)
    ref[i, pl.ds(start, CY), :] = value


def x_row(ref, i, y):
    return ref[i, pl.ds(y, CX, stride=CY), :]


def x_shifted(row, step, left, right):
    if step == 0:
        return row
    at = iota((CX, NZ), 0)
    if step == 1:
        return jnp.where(at == 0, left, roll(row, 1, 0))
    return jnp.where(at == CX - 1, right, roll(row, -1, 0))


def face_kernel(first_ref, last_ref, vel_ref, up_ref, down_ref):
    for ref, out, which in ((last_ref, up_ref, XP), (first_ref, down_ref, XM)):
        f = [ref[i] for i in range(19)]
        fs = relaxed(f, which, *moments(f))
        for n, i in enumerate(which):
            out[n] = fs[i]
        out[5] = jnp.zeros((CY, NZ), F32)
        out[5, 0:3, 0:PER] = vel_ref[...]


def collide_kernel(pop_ref, fs_ref):
    def body(x, carry):
        f = [plane_at(pop_ref, i, x) for i in range(19)]
        fs = relaxed(f, range(19), *moments(f))
        for i in range(19):
            put_plane(fs_ref, i, x, fs[i])
        return carry

    lax.fori_loop(0, CX, body, 0)


def row_kernel(fs_ref, mask_ref, id_ref, left_ref, right_ref, own_ref, up_ref, down_ref):
    shape = (CX, NZ)
    near, far = tables(left_ref[5], own_ref[5], right_ref[5], shape)
    for y, outward, missing, inner, out in ((CY - 1, YP, YM, CY - 2, up_ref), (0, YM, YP, 1, down_ref)):
        fs = [x_row(fs_ref, i, y) for i in range(19)]
        masks = [x_row(mask_ref, p, y) for p in range(2)]
        wall = wall_terms(velocity_of(id_ref[pl.ds(y, CX, stride=CY), :], near, far))
        f = [fs[0]]
        for i in range(1, 19):
            cx, cy, cz = DIRS[i]
            back = fs[opp(i)]
            if i in missing:
                moved = jnp.zeros(shape, F32)
            else:
                src_y = inner if i in outward else y
                moved = x_row(fs_ref, i, src_y) if i in outward else fs[i]
                if cx == 1:
                    moved = x_shifted(moved, 1, left_ref[XP.index(i), src_y : src_y + 1, :], None)
                elif cx == -1:
                    moved = x_shifted(moved, -1, None, right_ref[XM.index(i), src_y : src_y + 1, :])
            if cz != 0:
                if i not in missing:
                    moved = roll(moved, cz, 1)
                moved = jnp.where(z_edge(shape, cz), back, moved)
            f.append(jnp.where(bit_set(masks, opp(i)), back + wall[i], moved))
        rho, mom = moments(f)
        for n, i in enumerate(outward):
            out[n * CX : (n + 1) * CX, :] = fs[i]
            out[(5 + n) * CX : (6 + n) * CX, :] = f[i]
        for n, total in enumerate((rho, *mom)):
            out[(10 + n) * CX : (11 + n) * CX, :] = total
        for p in range(2):
            out[(14 + p) * CX : (15 + p) * CX, :] = masks[p].astype(F32)
        out[256:264, :] = jnp.zeros((8, NZ), F32)
        for i in outward:
            if DIRS[i][0] == 1:
                out[256:257, :] = left_ref[XP.index(i), y : y + 1, :]
            elif DIRS[i][0] == -1:
                out[257:258, :] = right_ref[XM.index(i), y : y + 1, :]


def arrive(fs, source, halo_row, masks, wall):
    shape = (CY, NZ)
    sub = iota(shape, 0)
    f = [fs[0]]
    for i in range(1, 19):
        cx, cy, cz = DIRS[i]
        back = fs[opp(i)]
        moved = source(i)
        if cy != 0:
            moved = roll(moved, cy, 0)
            edge = sub == (0 if cy == 1 else CY - 1)
            moved = jnp.where(edge, halo_row(i), moved)
        if cz != 0:
            moved = jnp.where(z_edge(shape, cz), back, roll(moved, cz, 1))
        f.append(jnp.where(bit_set(masks, opp(i)), back + wall[i], moved))
    return f


def first_step_kernel(fs_ref, mask_ref, id_ref, left_ref, right_ref, own_ref, f_ref, vel_ref, force_ref):
    shape = (CY, NZ)
    near, far = tables(left_ref[5], own_ref[5], right_ref[5], shape)

    def plane(x, source):
        fs = [plane_at(fs_ref, i, x) for i in range(19)]
        masks = [plane_at(mask_ref, p, x) for p in range(2)]
        start = x * CY if isinstance(x, int) else pl.multiple_of(x * CY, CY)
        vel = velocity_of(id_ref[pl.ds(start, CY), :], near, far)
        wall = wall_terms(vel)
        f = arrive(fs, source, lambda i: 0.0, masks, wall)
        for i in range(19):
            put_plane(f_ref, i, x, f[i])
        force = [jnp.zeros(shape, F32) for k in range(3)]
        for i in range(1, 19):
            term = jnp.where(bit_set(masks, i), 2.0 * (fs[i] - wall[i]), 0.0)
            for k in range(3):
                if DIRS[i][k] == 1:
                    force[k] = force[k] + term
                elif DIRS[i][k] == -1:
                    force[k] = force[k] - term
        for k in range(3):
            put_plane(vel_ref, k, x, vel[k])
            put_plane(force_ref, k, x, force[k])

    def inner(x, carry):
        plane(x, lambda i: plane_at(fs_ref, i, x - DIRS[i][0]))
        return carry

    plane(0, lambda i: left_ref[XP.index(i)] if i in XP else plane_at(fs_ref, i, 0 - DIRS[i][0]))
    lax.fori_loop(1, CX - 1, inner, 0)
    plane(CX - 1, lambda i: right_ref[XM.index(i)] if i in XM else plane_at(fs_ref, i, CX - 1 - DIRS[i][0]))


HI, LO = 6, 32


def second_step_kernel(
    fs_ref, f_ref, mask_ref, id_ref, force_ref, left_ref, right_ref, below_ref, above_ref,
    fs2_ref, halo_ref, up_ref, down_ref, mine_ref, fix_ref, a_ref, b_ref,
):
    shape = (CX, NZ)
    for side, (y, inward, outward, got) in enumerate(((0, YP, YM, below_ref), (CY - 1, YM, YP, above_ref))):
        masks = [got[(14 + p) * CX : (15 + p) * CX, :].astype(jnp.int32) for p in range(2)]
        rho = got[10 * CX : 11 * CX, :]
        mom = [got[(11 + k) * CX : (12 + k) * CX, :] for k in range(3)]
        for i in outward:
            cx, cy, cz = DIRS[i]
            moved = x_row(fs_ref, i, y)
            if cx == 1:
                moved = x_shifted(moved, 1, left_ref[XP.index(i), y : y + 1, :], None)
            elif cx == -1:
                moved = x_shifted(moved, -1, None, right_ref[XM.index(i), y : y + 1, :])
            held = bit_set(masks, opp(i))
            if cz != 0:
                moved = roll(moved, cz, 1)
                held = jnp.logical_or(held, z_edge(shape, cz))
            moved = jnp.where(held, 0.0, moved)
            rho = rho + moved
            for k in range(3):
                if DIRS[i][k] == 1:
                    mom[k] = mom[k] + moved
                elif DIRS[i][k] == -1:
                    mom[k] = mom[k] - moved
        f = {i: got[(5 + n) * CX : (6 + n) * CX, :] for n, i in enumerate(inward)}
        beyond = relaxed(f, inward, rho, mom)
        masks = [x_row(mask_ref, p, y) for p in range(2)]
        for n, i in enumerate(inward):
            halo_ref[side * 5 + n] = beyond[i]
            cx, cy, cz = DIRS[i]
            moved = x_shifted(got[n * CX : (n + 1) * CX, :], cx, got[256:257, :], got[257:258, :])
            held = bit_set(masks, opp(i))
            if cz != 0:
                moved = roll(moved, cz, 1)
                held = jnp.logical_or(held, z_edge(shape, cz))
            fix_ref[side * 5 + n] = jnp.where(held, 0.0, moved)

    sub = iota((CY, NZ), 0)

    def body(x, carry):
        f = [plane_at(f_ref, i, x) for i in range(19)]
        for side, inward, at in ((0, YP, 0), (1, YM, CY - 1)):
            for n, i in enumerate(inward):
                f[i] = f[i] + jnp.where(sub == at, fix_ref[side * 5 + n, pl.ds(x, 1), :], 0.0)
        fs = relaxed(f, range(19), *moments(f))
        masks = [plane_at(mask_ref, p, x) for p in range(2)]
        hits = [None, None, None]
        for i in range(19):
            put_plane(fs2_ref, i, x, fs[i])
            if i > 0:
                term = jnp.where(bit_set(masks, i), fs[i], 0.0)
                for k in range(3):
                    if DIRS[i][k] == 0:
                        continue
                    if hits[k] is None:
                        hits[k] = term
                    elif DIRS[i][k] == 1:
                        hits[k] = hits[k] + term
                    else:
                        hits[k] = hits[k] - term
        start = pl.multiple_of(x * CY, CY)
        lanes = pl.ds(pl.multiple_of(x * NZ, NZ), NZ)
        block, member = slots(id_ref[pl.ds(start, CY), :])
        slot = block * PER + member
        hi, lo = jnp.right_shift(slot, 5), jnp.bitwise_and(slot, LO - 1)
        at_hi = [hi == h for h in range(HI)]
        for k in range(3):
            force = plane_at(force_ref, k, x) + 2.0 * hits[k]
            coarse = force.astype(jnp.bfloat16).astype(F32)
            for part, value in enumerate((coarse, force - coarse)):
                for h in range(0, HI, 2):
                    both = jnp.concatenate(
                        [jnp.where(at_hi[h], value, 0.0), jnp.where(at_hi[h + 1], value, 0.0)], axis=0
                    )
                    for h2 in range(2):
                        row = ((part * 2 + h2) * 9 + (h // 2) * 3 + k) * CY
                        a_ref[row : row + CY, lanes] = both[h2 * CY : (h2 + 1) * CY]
        for v in range(0, LO, 2):
            both = jnp.concatenate(
                [jnp.where(lo == v, 1.0, 0.0), jnp.where(lo == v + 1, 1.0, 0.0)], axis=0
            )
            b_ref[v * CY : (v + 2) * CY, lanes] = both.astype(jnp.bfloat16)
        return carry

    lax.fori_loop(0, CX, body, 0)

    cross = lax.dot_general(
        a_ref[...].astype(jnp.bfloat16), b_ref[...], (((1,), (1,)), ((), ())), preferred_element_type=F32
    )
    cross = cross[: 18 * CY] + cross[18 * CY :]
    same = jnp.bitwise_and(iota(cross.shape, 0), CY - 1) == jnp.bitwise_and(iota(cross.shape, 1), CY - 1)
    cross = jnp.where(same, cross, 0.0)
    column, lane = iota((LO * CY, NZ), 0), iota((LO * CY, NZ), 1)
    sums = None
    for h2 in range(2):
        pick = (jnp.right_shift(column, 3) + h2 * LO == lane).astype(F32)
        part = jnp.dot(
            cross[h2 * 9 * CY : (h2 + 1) * 9 * CY], pick, preferred_element_type=F32, precision=lax.Precision.HIGHEST
        )
        sums = part if sums is None else sums + part
    terms = [[jnp.sum(sums[(b * 3 + k) * CY : (b * 3 + k + 1) * CY], axis=0, keepdims=True) for k in range(3)] for b in range(3)]

    for out, which, x, block, corners in (
        (up_ref, XP, CX - 1, 2, (7, 9)),
        (down_ref, XM, 0, 0, (10, 8)),
    ):
        for n, i in enumerate(which):
            out[n] = plane_at(fs2_ref, i, x)
        rows = [
            halo_ref[YP.index(corners[0]), x : x + 1, :],
            halo_ref[5 + YM.index(corners[1]), x : x + 1, :],
            *terms[block],
        ]
        packed = jnp.zeros((CY, NZ), F32)
        for n, row in enumerate(rows):
            packed = jnp.where(sub == n, row, packed)
        out[5] = packed
    packed = jnp.zeros((CY, NZ), F32)
    for n, row in enumerate(terms[1]):
        packed = jnp.where(sub == n + 2, row, packed)
    mine_ref[...] = packed


def halo_slot(i):
    return YP.index(i) if DIRS[i][1] == 1 else 5 + YM.index(i)


def inner_planes_kernel(fs_ref, halo_ref, mask_ref, vel_ref, out_ref):
    def body(x, carry):
        fs = [plane_at(fs_ref, i, x) for i in range(19)]
        masks = [plane_at(mask_ref, p, x) for p in range(2)]
        wall = wall_terms([plane_at(vel_ref, k, x) for k in range(3)])
        f = arrive(
            fs,
            lambda i: plane_at(fs_ref, i, x - DIRS[i][0]),
            lambda i: halo_ref[halo_slot(i), pl.ds(x - DIRS[i][0], 1), :],
            masks,
            wall,
        )
        for i in range(19):
            put_plane(out_ref, i, x, f[i])
        return carry

    lax.fori_loop(1, CX - 1, body, 0)
    for x in (0, CX - 1):
        for i in range(19):
            put_plane(out_ref, i, x, plane_at(fs_ref, i, x))


def edge_planes_kernel(
    fs_ref, halo_ref, mask_ref, vel_ref, left_ref, right_ref, mine_ref, whole_ref, out_ref, force_ref
):
    del whole_ref

    def edge(local, x, far_ref, far_dirs):
        fs = [fs_ref[i, local * CY : (local + 1) * CY, :] for i in range(19)]
        masks = [mask_ref[p, local * CY : (local + 1) * CY, :] for p in range(2)]
        wall = wall_terms([vel_ref[k, local * CY : (local + 1) * CY, :] for k in range(3)])

        def source(i):
            if i in far_dirs:
                return far_ref[far_dirs.index(i)]
            at = local - DIRS[i][0]
            return fs_ref[i, at * CY : (at + 1) * CY, :]

        def halo_row(i):
            if i in far_dirs:
                n = 0 if DIRS[i][1] == 1 else 1
                return far_ref[5, n : n + 1, :]
            at = x - DIRS[i][0]
            return halo_ref[halo_slot(i), at : at + 1, :]

        f = arrive(fs, source, halo_row, masks, wall)
        for i in range(19):
            out_ref[i] = f[i]

    @pl.when(pl.program_id(0) == 0)
    def _():
        edge(0, 0, left_ref, XP)
        total = mine_ref[...] + left_ref[5] + right_ref[5]
        force_ref[...] = total[2:5, 0:PER]

    @pl.when(pl.program_id(0) == 1)
    def _():
        edge(1, CX - 1, right_ref, XM)


def params(**more):
    return pltpu.CompilerParams(vmem_limit_bytes=VMEM_LIMIT, **more)


def cost(flops, nbytes):
    return pl.CostEstimate(flops=flops, bytes_accessed=nbytes, transcendentals=0)


def shape(*dims):
    return jax.ShapeDtypeStruct(dims, F32)


def shift(x, axis, by):
    count = lax.axis_size(axis)
    return lax.ppermute(x, axis, [(i, (i + by) % count) for i in range(count)])


def on_device(populations, link_mask, sphere_of_cell, sphere_velocity):
    pops = populations.reshape(19, ROWS, NZ)
    mask = link_mask.reshape(2, ROWS, NZ)
    ids = sphere_of_cell.reshape(ROWS, NZ)
    vel = sphere_velocity.reshape(3, PER)
    cells = ROWS * NZ
    xmsg = (6, CY, NZ)

    to_right, to_left = pl.pallas_call(
        face_kernel,
        grid=(1,),
        in_specs=[
            pl.BlockSpec((19, CY, NZ), lambda g: (0, 0, 0)),
            pl.BlockSpec((19, CY, NZ), lambda g: (0, CX - 1, 0)),
            pl.BlockSpec((3, PER), lambda g: (0, 0)),
        ],
        out_specs=[pl.BlockSpec(xmsg, lambda g: (0, 0, 0))] * 2,
        out_shape=[shape(*xmsg)] * 2,
        compiler_params=params(),
        name="faces",
    )(pops, pops, vel)
    left = shift(to_right, "row", 1)
    right = shift(to_left, "row", -1)

    fs1 = pl.pallas_call(
        collide_kernel,
        out_shape=shape(19, ROWS, NZ),
        compiler_params=params(),
        cost_estimate=cost(300 * cells, 38 * 4 * cells),
        name="collide",
    )(pops)

    up, down = pl.pallas_call(
        row_kernel,
        out_shape=[shape(YMSG, NZ)] * 2,
        compiler_params=params(),
        name="y_rows",
    )(fs1, mask, ids, left, right, to_right)
    below = shift(up, "col", 1)
    above = shift(down, "col", -1)

    f1, cell_vel, force1 = pl.pallas_call(
        first_step_kernel,
        out_shape=[shape(19, ROWS, NZ), shape(3, ROWS, NZ), shape(3, ROWS, NZ)],
        compiler_params=params(),
        cost_estimate=cost(500 * cells, 50 * 4 * cells),
        name="first_step",
    )(fs1, mask, ids, left, right, to_right)

    fs2, halo, to_right2, to_left2, mine = pl.pallas_call(
        second_step_kernel,
        out_shape=[shape(19, ROWS, NZ), shape(10, CX, NZ), shape(*xmsg), shape(*xmsg), shape(CY, NZ)],
        scratch_shapes=[
            pltpu.VMEM((10, CX, NZ), F32),
            pltpu.VMEM((2 * 18 * CY, CX * NZ), F32),
            pltpu.VMEM((LO * CY, CX * NZ), jnp.bfloat16),
        ],
        compiler_params=params(),
        name="second_step",
    )(fs1, f1, mask, ids, force1, left, right, below, above)
    left2 = shift(to_right2, "row", 1)
    right2 = shift(to_left2, "row", -1)

    inner = pl.pallas_call(
        inner_planes_kernel,
        out_shape=shape(19, ROWS, NZ),
        compiler_params=params(),
        cost_estimate=cost(300 * cells, 45 * 4 * cells),
        name="inner_planes",
    )(fs2, halo, mask, cell_vel)

    last = CX // 2 - 1
    whole = pl.BlockSpec(xmsg, lambda g: (0, 0, 0))
    out, force = pl.pallas_call(
        edge_planes_kernel,
        grid=(2,),
        in_specs=[
            pl.BlockSpec((19, 2 * CY, NZ), lambda g: (0, g * last, 0)),
            pl.BlockSpec((10, CX, NZ), lambda g: (0, 0, 0)),
            pl.BlockSpec((2, 2 * CY, NZ), lambda g: (0, g * last, 0)),
            pl.BlockSpec((3, 2 * CY, NZ), lambda g: (0, g * last, 0)),
            whole,
            whole,
            pl.BlockSpec((CY, NZ), lambda g: (0, 0)),
            pl.BlockSpec(memory_space=pl.ANY),
        ],
        out_specs=[
            pl.BlockSpec((19, CY, NZ), lambda g: (0, g * (CX - 1), 0)),
            pl.BlockSpec((3, PER), lambda g: (0, 0)),
        ],
        out_shape=[shape(19, ROWS, NZ), shape(3, PER)],
        input_output_aliases={7: 0},
        compiler_params=params(),
        name="edge_planes",
    )(fs2, halo, mask, cell_vel, left2, right2, mine, inner)

    return out.reshape(19, CX, CY, NZ), force.reshape(1, 3, PER)


def solution(mesh):
    in_specs = (
        P(None, "row", "col", None),
        P(None, "row", "col", None),
        P("row", "col", None),
        P("col", None, "row"),
    )
    out_specs = (P(None, "row", "col", None), P("col", None, "row"))
    return jax.shard_map(on_device, mesh=mesh, in_specs=in_specs, out_specs=out_specs, check_vma=False)
```

time: 633 us -> 59.9 us (0.09)
  local copies, waits for them, and re-layouts: 354 us -> 2.55 us
  other arithmetic: 176 us -> 0 us
  waiting for transfers between devices: 40.9 us -> 12 us
  starting transfers between devices: 58.2 us -> 35.6 us
  Pallas kernels: 0 us -> 8.5 us
    gather x3 -> x0, local copies, waits for them, and re-layouts: 304 us -> none  [on_device(): cell_u = [records[0, axis_n][cell_slot] for axis_n in range(3)]]
    scatter-add x1 -> x0, other arithmetic: 87.6 us -> none  [on_device(): jax.ops.segment_sum(force_rows, slot_flat, num_segments=records.shape[2])]
    add x4 -> x0, other arithmetic: 46.5 us -> none  [the longest x3 46.5 us: propagate(): link_force[axis_n] + lattice_dirs[index][axis_n] * transfer]
    ppermute x12 -> x6, waiting for transfers between devices: 40.9 us -> 12 us  [shift(): return lax.ppermute(x, axis, [(i, (i + by) % count) for i in range(count)])]
    unnamed x50 -> x0, other arithmetic: 27.7 us -> none
    ppermute x12 -> x6, starting transfers between devices: 58.2 us -> 35.6 us  [shift(): return lax.ppermute(x, axis, [(i, (i + by) % count) for i in range(count)])]
    concatenate x36 -> x0, local copies, waits for them, and re-layouts: 21.4 us -> none  [propagate(): moved = jnp.roll(moved, step_z, axis=2)]
    slice x34 -> x0, local copies, waits for them, and re-layouts: 15 us -> none  [the longest x30 13.7 us: propagate(): moved = jnp.roll(moved, step_z, axis=2)]
  transfers between devices with their start and end apart: 12 -> 6, of which waited for: 4 -> 3; matrix products, arithmetic and copies ran while one was open for 52% -> 0% of each run, Pallas kernels for 0% -> 8%
where the time goes in v1:
time: 59.9 us; the launch traced here: 59.4 us
  starting transfers between devices  35.6 us (59%)
  waiting for transfers between devices  12 us (20%)
  Pallas kernels  8.5 us (14%)
  local copies, waits for them, and re-layouts  2.55 us (4%)
  between operations  0.74 us (1%)
    ppermute x6, starting transfers between devices, shift(): return lax.ppermute(x, axis, [(i, (i + by) % count) for i in range(count)])  35.6 us
    ppermute x6, waiting for transfers between devices, shift(): return lax.ppermute(x, axis, [(i, (i + by) % count) for i in range(count)])  12 us
    unnamed x8, local copies, waits for them, and re-layouts  2.55 us
    pallas_call x1, Pallas kernels, on_device(): pl.pallas_call(second_step_kernel, out_shape=[shape(19, ROWS, NZ), shape(...  2.49 us
    pallas_call x1, Pallas kernels, on_device(): pl.pallas_call(inner_planes_kernel, out_shape=shape(19, ROWS, NZ), compil...  2.25 us
    pallas_call x1, Pallas kernels, on_device(): pl.pallas_call(first_step_kernel, out_shape=[shape(19, ROWS, NZ), shape(3...  1.79 us
  transfers between devices with their start and end apart: 6, of which 3 were waited for; matrix products, arithmetic and copies ran while one was open for 0% of the time, Pallas kernels for 8%

profile of v1, /device:TPU:56, one launch (start us, length us, event | category | flops | bytes accessed | tf_op | source)
XLA Modules:
  0.0 59.4 jit_solution(18035430227727058965)
XLA Ops:
  0.6 0.7 %copy.10 = f32[1,3,64]{2,1,0:T(4,128)S(1)} copy(f32[1,3,64]{2,0,1:T(1,128)} %param.7) | data formatting | bytes 1536
  1.3 0.0 copy-start
  1.3 1.3 %copy-done = f32[19,16,8,128]{3,2,1,0:T(8,128)S(1)} copy-done((f32[19,16,8,128]{3,2,1,0:T(8,128)S(1)}, f32[19,16,8,128]{3,2,1,0:T(8,128)}, u32[]{:S(2)}) %copy-start) | copy-done | bytes 1245208
  2.7 9.5 %collective-permute-start.1 = (f32[6,8,128]{2,1,0:T(8,128)S(1)}, f32[6,8,128]{2,1,0:T(8,128)S(1)}, u32[]{:S(2)}, u32[]{:S(2)}) collective-permute-start(f32[6,8,128]{2,1,0:T(8,128)S(1)} %get-tuple-element.17), channel_id=1, source_target_pairs={{0,744},{24,0},{48,24},{72,48},{96,72},{120,96},{144,120},{168,144... | collective-permute-start | bytes 73736 | tf_op jit(solution)/shard_map/ppermute | solution.py:489
  12.2 0.0 copy-start.1
  12.2 0.0 copy-start.2
  12.2 2.1 %collective-permute-start = (f32[6,8,128]{2,1,0:T(8,128)S(1)}, f32[6,8,128]{2,1,0:T(8,128)S(1)}, u32[]{:S(2)}, u32[]{:S(2)}) collective-permute-start(f32[6,8,128]{2,1,0:T(8,128)S(1)} %get-tuple-element.16.own_ref), channel_id=1, source_target_pairs={{0,24},{24,48},{48,72},{72,96},{96,120},{120,144},{144,168},{168,1... | collective-permute-start | bytes 73736 | tf_op jit(solution)/shard_map/ppermute | solution.py:489
  14.3 0.8 %collide.1.fs_ref = f32[19,128,128]{2,1,0:T(8,128)S(1)} custom-call(f32[19,128,128]{2,1,0:T(8,128)S(1)} %bitcast.10), custom_call_target="tpu_custom_call" | custom-call | flops 4915200 | bytes 2490368 | tf_op jit(solution)/shard_map/collide/pallas_call | solution.py:516
  15.1 0.0 collective-permute-done.1.right_ref
  15.1 6.3 %collective-permute-done.left_ref = f32[6,8,128]{2,1,0:T(8,128)S(1)} collective-permute-done((f32[6,8,128]{2,1,0:T(8,128)S(1)}, f32[6,8,128]{2,1,0:T(8,128)S(1)}, u32[]{:S(2)}, u32[]{:S(2)}) %collective-permute-start) | collective-permute-done | bytes 24608 | tf_op jit(solution)/shard_map/ppermute | solution.py:489
  21.4 0.0 copy-done.1
  21.4 0.0 copy-done.2
  21.4 0.2 y_rows.1
  21.6 10.6 %collective-permute-start.2 = (f32[264,128]{1,0:T(8,128)S(1)}, f32[264,128]{1,0:T(8,128)S(1)}, u32[]{:S(2)}, u32[]{:S(2)}) collective-permute-start(f32[264,128]{1,0:T(8,128)S(1)} %get-tuple-element.20), channel_id=1, source_target_pairs={{0,1},{1,2},{2,3},{3,4},{4,5},{5,6},{6,7},{7,8},{8,9},{9,10},{10,1... | collective-permute-start | bytes 405512 | tf_op jit(solution)/shard_map/ppermute | solution.py:489
  32.3 3.9 %collective-permute-start.3 = (f32[264,128]{1,0:T(8,128)S(1)}, f32[264,128]{1,0:T(8,128)S(1)}, u32[]{:S(2)}, u32[]{:S(2)}) collective-permute-start(f32[264,128]{1,0:T(8,128)S(1)} %get-tuple-element.21), channel_id=1, source_target_pairs={{0,23},{1,0},{2,1},{3,2},{4,3},{5,4},{6,5},{7,6},{8,7},{9,8},{10,9... | collective-permute-start | bytes 405512 | tf_op jit(solution)/shard_map/ppermute | solution.py:489
  36.2 1.8 %first_step.1 = (f32[19,128,128]{2,1,0:T(8,128)S(1)}, f32[3,128,128]{2,1,0:T(8,128)S(1)}, f32[3,128,128]{2,1,0:T(8,128)S(1)}) custom-call(f32[19,128,128]{2,1,0:T(8,128)S(1)} %collide.1.fs_ref, s32[2,128,128]{2,1,0:T(8,128)S(1)} %bitcast.12, s32[128,128]{1,0:T(8,128)S(1)} %bitcast.17, f32[6,8,128]{2,1,0:T(8,128)S(1)} %collective-permute-done.left_ref, ...), custom_call_target="tpu_custom_call" | custom-call | flops 8192000 | bytes 3276800 | tf_op jit(solution)/shard_map/first_step/pallas_call | solution.py:533
  38.0 3.9 %collective-permute-done.2.below_ref = f32[264,128]{1,0:T(8,128)S(1)} collective-permute-done((f32[264,128]{1,0:T(8,128)S(1)}, f32[264,128]{1,0:T(8,128)S(1)}, u32[]{:S(2)}, u32[]{:S(2)}) %collective-permute-start.2) | collective-permute-done | bytes 135200 | tf_op jit(solution)/shard_map/ppermute | solution.py:489
  42.0 1.7 %collective-permute-done.3.above_ref = f32[264,128]{1,0:T(8,128)S(1)} collective-permute-done((f32[264,128]{1,0:T(8,128)S(1)}, f32[264,128]{1,0:T(8,128)S(1)}, u32[]{:S(2)}, u32[]{:S(2)}) %collective-permute-start.3) | collective-permute-done | bytes 135200 | tf_op jit(solution)/shard_map/ppermute | solution.py:489
  43.7 2.5 %second_step.1 = (f32[19,128,128]{2,1,0:T(8,128)S(1)}, f32[10,16,128]{2,1,0:T(8,128)S(1)}, f32[6,8,128]{2,1,0:T(8,128)S(1)}, f32[6,8,128]{2,1,0:T(8,128)S(1)}, f32[8,128]{1,0:T(8,128)S(1)}) custom-call(f32[19,128,128]{2,1,0:T(8,128)S(1)} %collide.1.fs_ref, f32[19,128,128]{2,1,0:T(8,128)S(1)} %get-tuple-element.18.f_ref, s32[2,128,128]{2,1,0:T(8,128)S(1)} %bitcast.13, ...), custom_call_target="tpu_custom_call" | custom-call | tf_op jit(solution)/shard_map/second_step/pallas_call | solution.py:541
  46.2 1.9 %collective-permute-start.4 = (f32[6,8,128]{2,1,0:T(8,128)S(1)}, f32[6,8,128]{2,1,0:T(8,128)S(1)}, u32[]{:S(2)}, u32[]{:S(2)}) collective-permute-start(f32[6,8,128]{2,1,0:T(8,128)S(1)} %get-tuple-element.25), channel_id=1, source_target_pairs={{0,24},{24,48},{48,72},{72,96},{96,120},{120,144},{144,168},{168,1... | collective-permute-start | bytes 73736 | tf_op jit(solution)/shard_map/ppermute | solution.py:489
  48.1 7.5 %collective-permute-start.5 = (f32[6,8,128]{2,1,0:T(8,128)S(1)}, f32[6,8,128]{2,1,0:T(8,128)S(1)}, u32[]{:S(2)}, u32[]{:S(2)}) collective-permute-start(f32[6,8,128]{2,1,0:T(8,128)S(1)} %get-tuple-element.26), channel_id=1, source_target_pairs={{0,744},{24,0},{48,24},{72,48},{96,72},{120,96},{144,120},{168,144... | collective-permute-start | bytes 73736 | tf_op jit(solution)/shard_map/ppermute | solution.py:489
  55.6 2.3 %inner_planes.1.whole_ref = f32[19,128,128]{2,1,0:T(8,128)} custom-call(f32[19,128,128]{2,1,0:T(8,128)S(1)} %get-tuple-element.22.fs_ref, f32[10,16,128]{2,1,0:T(8,128)S(1)} %get-tuple-element.23.halo_ref, s32[2,128,128]{2,1,0:T(8,128)S(1)} %bitcast.14, f32[3,128,128]{2,1,0:T(8,128)S(1)} %get-tuple-element.24.vel_ref), custom_call_target="tpu_custom_call" | custom-call | flops 4915200 | bytes 2949120 | tf_op jit(solution)/shard_map/inner_planes/pallas_call | solution.py:555
  57.9 0.0 collective-permute-done.4.left_ref
  57.9 0.0 collective-permute-done.5.right_ref
  57.9 0.9 %edge_planes.1 = (f32[19,128,128]{2,1,0:T(8,128)}, f32[3,64]{1,0:T(4,128)S(1)}) custom-call(f32[19,128,128]{2,1,0:T(8,128)S(1)} %get-tuple-element.22.fs_ref, f32[10,16,128]{2,1,0:T(8,128)S(1)} %get-tuple-element.23.halo_ref, s32[2,128,128]{2,1,0:T(8,128)S(1)} %bitcast.15, ...), custom_call_target="tpu_custom_call", output_to_operand_aliasing={{0}: (7, {})} | custom-call | tf_op jit(solution)/shard_map/edge_planes/pallas_call | solution.py:565
  58.8 0.6 copy.7
  (1 shorter events, 0.0 us)
Async XLA Ops:
  1.3 1.3 %copy-start = (f32[19,16,8,128]{3,2,1,0:T(8,128)S(1)}, f32[19,16,8,128]{3,2,1,0:T(8,128)}, u32[]{:S(2)}) copy-start(f32[19,16,8,128]{3,2,1,0:T(8,128)} %param.4) | copy-start | bytes 3735556
  2.7 12.4 %collective-permute-start.1 = (f32[6,8,128]{2,1,0:T(8,128)S(1)}, f32[6,8,128]{2,1,0:T(8,128)S(1)}, u32[]{:S(2)}, u32[]{:S(2)}) collective-permute-start(f32[6,8,128]{2,1,0:T(8,128)S(1)} %get-tuple-element.17), channel_id=1, source_target_pairs={{0,744},{24,0},{48,24},{72,48},{96,72},{120,96},{144,120},{168,144... | collective-permute-start | bytes 73736 | tf_op jit(solution)/shard_map/ppermute | solution.py:489
  12.2 9.2 %copy-start.1 = (s32[2,16,8,128]{3,2,1,0:T(8,128)S(1)}, s32[2,16,8,128]{3,2,1,0:T(8,128)}, u32[]{:S(2)}) copy-start(s32[2,16,8,128]{3,2,1,0:T(8,128)} %param.5) | copy-start | bytes 393220
  12.2 9.2 %copy-start.2 = (s32[16,8,128]{2,1,0:T(8,128)S(1)}, s32[16,8,128]{2,1,0:T(8,128)}, u32[]{:S(2)}) copy-start(s32[16,8,128]{2,1,0:T(8,128)} %param.6) | copy-start | bytes 196612
  12.2 9.2 %collective-permute-start = (f32[6,8,128]{2,1,0:T(8,128)S(1)}, f32[6,8,128]{2,1,0:T(8,128)S(1)}, u32[]{:S(2)}, u32[]{:S(2)}) collective-permute-start(f32[6,8,128]{2,1,0:T(8,128)S(1)} %get-tuple-element.16.own_ref), channel_id=1, source_target_pairs={{0,24},{24,48},{48,72},{72,96},{96,120},{120,144},{144,168},{168,1... | collective-permute-start | bytes 73736 | tf_op jit(solution)/shard_map/ppermute | solution.py:489
  21.6 20.3 %collective-permute-start.2 = (f32[264,128]{1,0:T(8,128)S(1)}, f32[264,128]{1,0:T(8,128)S(1)}, u32[]{:S(2)}, u32[]{:S(2)}) collective-permute-start(f32[264,128]{1,0:T(8,128)S(1)} %get-tuple-element.20), channel_id=1, source_target_pairs={{0,1},{1,2},{2,3},{3,4},{4,5},{5,6},{6,7},{7,8},{8,9},{9,10},{10,1... | collective-permute-start | bytes 405512 | tf_op jit(solution)/shard_map/ppermute | solution.py:489
  32.3 11.4 %collective-permute-start.3 = (f32[264,128]{1,0:T(8,128)S(1)}, f32[264,128]{1,0:T(8,128)S(1)}, u32[]{:S(2)}, u32[]{:S(2)}) collective-permute-start(f32[264,128]{1,0:T(8,128)S(1)} %get-tuple-element.21), channel_id=1, source_target_pairs={{0,23},{1,0},{2,1},{3,2},{4,3},{5,4},{6,5},{7,6},{8,7},{9,8},{10,9... | collective-permute-start | bytes 405512 | tf_op jit(solution)/shard_map/ppermute | solution.py:489
  46.2 11.7 %collective-permute-start.4 = (f32[6,8,128]{2,1,0:T(8,128)S(1)}, f32[6,8,128]{2,1,0:T(8,128)S(1)}, u32[]{:S(2)}, u32[]{:S(2)}) collective-permute-start(f32[6,8,128]{2,1,0:T(8,128)S(1)} %get-tuple-element.25), channel_id=1, source_target_pairs={{0,24},{24,48},{48,72},{72,96},{96,120},{120,144},{144,168},{168,1... | collective-permute-start | bytes 73736 | tf_op jit(solution)/shard_map/ppermute | solution.py:489
  48.1 9.8 %collective-permute-start.5 = (f32[6,8,128]{2,1,0:T(8,128)S(1)}, f32[6,8,128]{2,1,0:T(8,128)S(1)}, u32[]{:S(2)}, u32[]{:S(2)}) collective-permute-start(f32[6,8,128]{2,1,0:T(8,128)S(1)} %get-tuple-element.26), channel_id=1, source_target_pairs={{0,744},{24,0},{48,24},{72,48},{96,72},{120,96},{144,120},{168,144... | collective-permute-start | bytes 73736 | tf_op jit(solution)/shard_map/ppermute | solution.py:489

commit v2 on v1

v2 whole, which is shorter than its diff:
```python
import jax
import jax.numpy as jnp
from jax import lax
from jax.experimental import pallas as pl
from jax.experimental.pallas import tpu as pltpu
from jax.sharding import PartitionSpec as P

DIRS = (
    (0, 0, 0),
    (1, 0, 0),
    (-1, 0, 0),
    (0, 1, 0),
    (0, -1, 0),
    (0, 0, 1),
    (0, 0, -1),
    (1, 1, 0),
    (-1, -1, 0),
    (1, -1, 0),
    (-1, 1, 0),
    (1, 0, 1),
    (-1, 0, -1),
    (1, 0, -1),
    (-1, 0, 1),
    (0, 1, 1),
    (0, -1, -1),
    (0, 1, -1),
    (0, -1, 1),
)
WEIGHTS = (1.0 / 3.0,) + (1.0 / 18.0,) * 6 + (1.0 / 36.0,) * 12
RELAX = 1.25
F32 = jnp.float32
CX, CY, NZ, PER = 16, 8, 128, 64
ROWS = CX * CY
XP = tuple(i for i in range(19) if DIRS[i][0] == 1)
XM = tuple(i for i in range(19) if DIRS[i][0] == -1)
YP = tuple(i for i in range(19) if DIRS[i][1] == 1)
YM = tuple(i for i in range(19) if DIRS[i][1] == -1)
YMSG = 264
VMEM_LIMIT = 40 * 1024 * 1024


def opp(i):
    return 0 if i == 0 else (i + 1 if i % 2 == 1 else i - 1)


def project(direction, vec):
    total = None
    for k in range(3):
        if direction[k] != 0:
            term = vec[k] if direction[k] == 1 else -vec[k]
            total = term if total is None else total + term
    return total


def bit_set(masks, j):
    return jnp.bitwise_and(masks[(j - 1) // 9], 1 << ((j - 1) % 9)) != 0


def wall_terms(vel):
    terms = [None] * 19
    for i in range(1, 19, 2):
        along = (6.0 * WEIGHTS[i]) * project(DIRS[i], vel)
        terms[i] = along
        terms[i + 1] = -along
    return terms


def moments(f):
    rho = f[0]
    for i in range(1, 19):
        rho = rho + f[i]
    mom = []
    for k in range(3):
        total = None
        for i in range(19):
            if DIRS[i][k] != 0:
                if total is None:
                    total = f[i]
                elif DIRS[i][k] == 1:
                    total = total + f[i]
                else:
                    total = total - f[i]
        mom.append(total)
    return rho, mom


def relaxed(f, which, rho, mom):
    inv = 1.0 / rho
    u = [m * inv for m in mom]
    base = 1.0 - 1.5 * (u[0] * u[0] + u[1] * u[1] + u[2] * u[2])
    out = {}
    scaled = {w: (RELAX * w) * rho for w in sorted({WEIGHTS[i] for i in which})}
    for i in which:
        if i == 0:
            shape = base
        else:
            along = project(DIRS[i], u)
            shape = base + along * (3.0 + 4.5 * along)
        out[i] = (1.0 - RELAX) * f[i] + scaled[WEIGHTS[i]] * shape
    return out


def iota(shape, dim):
    return lax.broadcasted_iota(jnp.int32, shape, dim)


def roll(x, by, axis):
    return pltpu.roll(x, by % x.shape[axis], axis)


def slots(ids):
    count = lax.axis_size("row")
    block = jnp.right_shift(ids, 6) - lax.axis_index("row") + 1
    block = jnp.where(block < 0, block + count, block)
    block = jnp.where(block >= count, block - count, block)
    return block, jnp.bitwise_and(ids, PER - 1)


def tables(left, own, right, shape):
    low = iota((8, NZ), 1) < PER
    pair = jnp.where(low, left, roll(own, PER, 1))
    near = [jnp.broadcast_to(pair[k : k + 1], shape) for k in range(3)]
    far = [jnp.broadcast_to(right[k : k + 1], shape) for k in range(3)]
    return near, far


def velocity_of(ids, near, far):
    block, member = slots(ids)
    index = jnp.where(block == 1, member + PER, member)
    is_far = block == 2
    out = []
    for k in range(3):
        a = jnp.take_along_axis(near[k], index, axis=1, mode="promise_in_bounds")
        b = jnp.take_along_axis(far[k], index, axis=1, mode="promise_in_bounds")
        out.append(jnp.where(is_far, b, a))
    return out


def z_edge(shape, step):
    return iota(shape, 1) == (0 if step == 1 else NZ - 1)


def plane_at(ref, i, x):
    start = x * CY if isinstance(x, int) else pl.multiple_of(x * CY, CY)
    return ref[i, pl.ds(start, CY), :]


def put_plane(ref, i, x, value):
    start = x * CY if isinstance(x, int) else pl.multiple_of(x * CY, CY)
    ref[i, pl.ds(start, CY), :] = value


def x_row(ref, i, y):
    return ref[i, pl.ds(y, CX, stride=CY), :]


def x_shifted(row, step, left, right):
    if step == 0:
        return row
    at = iota((CX, NZ), 0)
    if step == 1:
        return jnp.where(at == 0, left, roll(row, 1, 0))
    return jnp.where(at == CX - 1, right, roll(row, -1, 0))


def even_row():
    return lax.rem(lax.axis_index("row"), 2) == 0


class Either:
    def __init__(self, even, if_even, if_odd):
        self.even, self.if_even, self.if_odd = even, if_even, if_odd

    def __getitem__(self, at):
        return jnp.where(self.even, self.if_even[at], self.if_odd[at])


def neighbours(inner_ref, outer_ref):
    even = even_row()
    return Either(even, outer_ref, inner_ref), Either(even, inner_ref, outer_ref)


def put_messages(inner_ref, outer_ref, to_right, to_left):
    even = even_row()
    for n in range(6):
        inner_ref[n] = jnp.where(even, to_right[n], to_left[n])
        outer_ref[n] = jnp.where(even, to_left[n], to_right[n])


def face_kernel(pop_ref, vel_ref, inner_ref, outer_ref, face_ref, held_ref, sems):
    copies = [
        pltpu.make_async_copy(pop_ref.at[:, pl.ds(ROWS - CY, CY), :], face_ref.at[0], sems.at[0]),
        pltpu.make_async_copy(pop_ref.at[:, pl.ds(0, CY), :], face_ref.at[1], sems.at[1]),
        pltpu.make_async_copy(vel_ref, held_ref, sems.at[2]),
    ]
    for copy in copies:
        copy.start()
    messages = []
    for side, which in enumerate((XP, XM)):
        copies[side].wait()
        f = [face_ref[side, i] for i in range(19)]
        fs = relaxed(f, which, *moments(f))
        messages.append([fs[i] for i in which] + [jnp.zeros((CY, NZ), F32)])
    put_messages(inner_ref, outer_ref, *messages)
    copies[2].wait()
    for out in (inner_ref, outer_ref):
        for k in range(3):
            out[5, k : k + 1, 0:PER] = held_ref[k]


def collide_kernel(pop_ref, fs_ref):
    def body(x, carry):
        f = [plane_at(pop_ref, i, x) for i in range(19)]
        fs = relaxed(f, range(19), *moments(f))
        for i in range(19):
            put_plane(fs_ref, i, x, fs[i])
        return carry

    lax.fori_loop(0, CX, body, 0)


def row_kernel(fs_ref, mask_ref, id_ref, inner_ref, outer_ref, own_ref, up_ref, down_ref):
    left_ref, right_ref = neighbours(inner_ref, outer_ref)
    shape = (CX, NZ)
    near, far = tables(left_ref[5], own_ref[5], right_ref[5], shape)
    for y, outward, missing, next_y, out in ((CY - 1, YP, YM, CY - 2, up_ref), (0, YM, YP, 1, down_ref)):
        fs = [x_row(fs_ref, i, y) for i in range(19)]
        masks = [x_row(mask_ref, p, y) for p in range(2)]
        wall = wall_terms(velocity_of(id_ref[pl.ds(y, CX, stride=CY), :], near, far))
        f = [fs[0]]
        for i in range(1, 19):
            cx, cy, cz = DIRS[i]
            back = fs[opp(i)]
            if i in missing:
                moved = jnp.zeros(shape, F32)
            else:
                src_y = next_y if i in outward else y
                moved = x_row(fs_ref, i, src_y) if i in outward else fs[i]
                if cx == 1:
                    moved = x_shifted(moved, 1, left_ref[XP.index(i), src_y : src_y + 1, :], None)
                elif cx == -1:
                    moved = x_shifted(moved, -1, None, right_ref[XM.index(i), src_y : src_y + 1, :])
            if cz != 0:
                if i not in missing:
                    moved = roll(moved, cz, 1)
                moved = jnp.where(z_edge(shape, cz), back, moved)
            f.append(jnp.where(bit_set(masks, opp(i)), back + wall[i], moved))
        rho, mom = moments(f)
        for n, i in enumerate(outward):
            out[n * CX : (n + 1) * CX, :] = fs[i]
            out[(5 + n) * CX : (6 + n) * CX, :] = f[i]
        for n, total in enumerate((rho, *mom)):
            out[(10 + n) * CX : (11 + n) * CX, :] = total
        for p in range(2):
            out[(14 + p) * CX : (15 + p) * CX, :] = masks[p].astype(F32)
        out[256:264, :] = jnp.zeros((8, NZ), F32)
        for i in outward:
            if DIRS[i][0] == 1:
                out[256:257, :] = left_ref[XP.index(i), y : y + 1, :]
            elif DIRS[i][0] == -1:
                out[257:258, :] = right_ref[XM.index(i), y : y + 1, :]


def arrive(fs, source, halo_row, masks, wall):
    shape = (CY, NZ)
    sub = iota(shape, 0)
    f = [fs[0]]
    for i in range(1, 19):
        cx, cy, cz = DIRS[i]
        back = fs[opp(i)]
        moved = source(i)
        if cy != 0:
            moved = roll(moved, cy, 0)
            edge = sub == (0 if cy == 1 else CY - 1)
            moved = jnp.where(edge, halo_row(i), moved)
        if cz != 0:
            moved = jnp.where(z_edge(shape, cz), back, roll(moved, cz, 1))
        f.append(jnp.where(bit_set(masks, opp(i)), back + wall[i], moved))
    return f


HI, LO = 6, 32


def add_hits(masks, values):
    total = [None, None, None]
    for i in range(1, 19):
        term = jnp.where(bit_set(masks, i), values(i), 0.0)
        for k in range(3):
            if DIRS[i][k] != 0:
                if total[k] is None:
                    total[k] = term
                elif DIRS[i][k] == 1:
                    total[k] = total[k] + term
                else:
                    total[k] = total[k] - term
    return [2.0 * t for t in total]


def put_cells(a_ref, b_ref, lanes, ids, force):
    block, member = slots(ids)
    slot = block * PER + member
    hi, lo = jnp.right_shift(slot, 5), jnp.bitwise_and(slot, LO - 1)
    at_hi = [hi == h for h in range(HI)]
    for k in range(3):
        coarse = force[k].astype(jnp.bfloat16).astype(F32)
        for part, value in enumerate((coarse, force[k] - coarse)):
            for h in range(HI):
                row = ((part * 2 + h % 2) * 9 + (h // 2) * 3 + k) * CY
                a_ref[row : row + CY, lanes] = jnp.where(at_hi[h], value, 0.0)
    for v in range(0, LO, 2):
        both = jnp.concatenate([jnp.where(lo == v, 1.0, 0.0), jnp.where(lo == v + 1, 1.0, 0.0)], axis=0)
        b_ref[v * CY : (v + 2) * CY, lanes] = both.astype(jnp.bfloat16)


def sphere_sums(a_ref, b_ref):
    cross = lax.dot_general(
        a_ref[...].astype(jnp.bfloat16), b_ref[...], (((1,), (1,)), ((), ())), preferred_element_type=F32
    )
    cross = cross[: 18 * CY] + cross[18 * CY :]
    same = jnp.bitwise_and(iota(cross.shape, 0), CY - 1) == jnp.bitwise_and(iota(cross.shape, 1), CY - 1)
    cross = jnp.where(same, cross, 0.0)
    column, lane = iota((LO * CY, NZ), 0), iota((LO * CY, NZ), 1)
    sums = None
    for h2 in range(2):
        pick = (jnp.right_shift(column, 3) + h2 * LO == lane).astype(F32)
        part = jnp.dot(
            cross[h2 * 9 * CY : (h2 + 1) * 9 * CY], pick, preferred_element_type=F32, precision=lax.Precision.HIGHEST
        )
        sums = part if sums is None else sums + part
    return [jnp.sum(sums[n * CY : (n + 1) * CY], axis=0, keepdims=True) for n in range(9)]


def first_step_kernel(
    fs_ref, mask_ref, id_ref, inner_ref, outer_ref, own_ref, f_ref, fs2_ref, vel_ref, sum_ref, a_ref, b_ref
):
    left_ref, right_ref = neighbours(inner_ref, outer_ref)
    shape = (CY, NZ)
    near, far = tables(left_ref[5], own_ref[5], right_ref[5], shape)
    sub = iota(shape, 0)
    inside = jnp.logical_and(sub > 0, sub < CY - 1)

    def plane(x, source):
        fs = [plane_at(fs_ref, i, x) for i in range(19)]
        masks = [plane_at(mask_ref, p, x) for p in range(2)]
        start, first = (x * CY, x * NZ) if isinstance(x, int) else (pl.multiple_of(x * CY, CY), pl.multiple_of(x * NZ, NZ))
        ids = id_ref[pl.ds(start, CY), :]
        vel = velocity_of(ids, near, far)
        wall = wall_terms(vel)
        force = add_hits(masks, lambda i: fs[i] - wall[i])
        f = arrive(fs, source, lambda i: 0.0, masks, wall)
        for i in range(19):
            put_plane(f_ref, i, x, f[i])
        fs2 = relaxed(f, range(19), *moments(f))
        for i in range(19):
            put_plane(fs2_ref, i, x, fs2[i])
        more = add_hits(masks, lambda i: fs2[i])
        force = [force[k] + jnp.where(inside, more[k], 0.0) for k in range(3)]
        for k in range(3):
            put_plane(vel_ref, k, x, vel[k])
        put_cells(a_ref, b_ref, pl.ds(first, NZ), ids, force)

    def inner(x, carry):
        plane(x, lambda i: plane_at(fs_ref, i, x - DIRS[i][0]))
        return carry

    plane(0, lambda i: left_ref[XP.index(i)] if i in XP else plane_at(fs_ref, i, 0 - DIRS[i][0]))
    lax.fori_loop(1, CX - 1, inner, 0)
    plane(CX - 1, lambda i: right_ref[XM.index(i)] if i in XM else plane_at(fs_ref, i, CX - 1 - DIRS[i][0]))
    sum_ref[...] = jnp.zeros(sum_ref.shape, F32)
    for n, row in enumerate(sphere_sums(a_ref, b_ref)):
        sum_ref[n : n + 1, :] = row


def second_step_kernel(
    fs_ref, f_ref, fs2_ref, mask_ref, id_ref, sum_ref, inner_ref, outer_ref, below_ref, above_ref,
    row_ref, halo_ref, to_inner_ref, to_outer_ref, mine_ref, a_ref, b_ref,
):
    left_ref, right_ref = neighbours(inner_ref, outer_ref)
    shape = (CX, NZ)
    for side, (y, inward, outward, got) in enumerate(((0, YP, YM, below_ref), (CY - 1, YM, YP, above_ref))):
        masks = [got[(14 + p) * CX : (15 + p) * CX, :].astype(jnp.int32) for p in range(2)]
        rho = got[10 * CX : 11 * CX, :]
        mom = [got[(11 + k) * CX : (12 + k) * CX, :] for k in range(3)]
        for i in outward:
            cx, cy, cz = DIRS[i]
            moved = x_row(fs_ref, i, y)
            if cx == 1:
                moved = x_shifted(moved, 1, left_ref[XP.index(i), y : y + 1, :], None)
            elif cx == -1:
                moved = x_shifted(moved, -1, None, right_ref[XM.index(i), y : y + 1, :])
            held = bit_set(masks, opp(i))
            if cz != 0:
                moved = roll(moved, cz, 1)
                held = jnp.logical_or(held, z_edge(shape, cz))
            moved = jnp.where(held, 0.0, moved)
            rho = rho + moved
            for k in range(3):
                if DIRS[i][k] == 1:
                    mom[k] = mom[k] + moved
                elif DIRS[i][k] == -1:
                    mom[k] = mom[k] - moved
        beyond = relaxed({i: got[(5 + n) * CX : (6 + n) * CX, :] for n, i in enumerate(inward)}, inward, rho, mom)
        for n, i in enumerate(inward):
            halo_ref[side * 5 + n] = beyond[i]

        masks = [x_row(mask_ref, p, y) for p in range(2)]
        f = [x_row(f_ref, i, y) for i in range(19)]
        for n, i in enumerate(inward):
            cx, cy, cz = DIRS[i]
            moved = x_shifted(got[n * CX : (n + 1) * CX, :], cx, got[256:257, :], got[257:258, :])
            held = bit_set(masks, opp(i))
            if cz != 0:
                moved = roll(moved, cz, 1)
                held = jnp.logical_or(held, z_edge(shape, cz))
            f[i] = f[i] + jnp.where(held, 0.0, moved)
        fs = relaxed(f, range(19), *moments(f))
        for i in range(19):
            row_ref[i, side * CX : (side + 1) * CX, :] = fs[i]
        force = add_hits(masks, lambda i: fs[i])
        ids = id_ref[pl.ds(y, CX, stride=CY), :]
        for half in range(2):
            part = slice(half * CY, (half + 1) * CY)
            lanes = slice((side * 2 + half) * NZ, (side * 2 + half + 1) * NZ)
            put_cells(a_ref, b_ref, lanes, ids[part], [t[part] for t in force])

    sub = iota((CY, NZ), 0)
    terms = [row + sum_ref[n : n + 1, :] for n, row in enumerate(sphere_sums(a_ref, b_ref))]
    messages = []
    for which, x, block, corners in ((XP, CX - 1, 2, (7, 9)), (XM, 0, 0, (10, 8))):
        planes = []
        for i in which:
            value = plane_at(fs2_ref, i, x)
            value = jnp.where(sub == 0, row_ref[i, x : x + 1, :], value)
            planes.append(jnp.where(sub == CY - 1, row_ref[i, CX + x : CX + x + 1, :], value))
        rows = [
            halo_ref[YP.index(corners[0]), x : x + 1, :],
            halo_ref[5 + YM.index(corners[1]), x : x + 1, :],
            *terms[block * 3 : block * 3 + 3],
        ]
        packed = jnp.zeros((CY, NZ), F32)
        for n, row in enumerate(rows):
            packed = jnp.where(sub == n, row, packed)
        messages.append(planes + [packed])
    put_messages(to_inner_ref, to_outer_ref, *messages)
    packed = jnp.zeros((CY, NZ), F32)
    for n, row in enumerate(terms[3:6]):
        packed = jnp.where(sub == n + 2, row, packed)
    mine_ref[...] = packed


def halo_slot(i):
    return YP.index(i) if DIRS[i][1] == 1 else 5 + YM.index(i)


def inner_planes_kernel(fs_ref, row_ref, halo_ref, mask_ref, vel_ref, out_ref, edge_ref, all_ref, made_ref, sems):
    for i in range(19):
        all_ref[i] = fs_ref[i]
        all_ref[i, pl.ds(0, CX, stride=CY), :] = row_ref[i, 0:CX, :]
        all_ref[i, pl.ds(CY - 1, CX, stride=CY), :] = row_ref[i, CX : 2 * CX, :]
        edge_ref[i, 0 : 2 * CY, :] = all_ref[i, 0 : 2 * CY, :]
        edge_ref[i, 2 * CY : 4 * CY, :] = all_ref[i, ROWS - 2 * CY : ROWS, :]

    def copy(x):
        rows = pl.ds(pl.multiple_of(x * CY, CY), CY)
        return pltpu.make_async_copy(made_ref.at[:, rows, :], out_ref.at[:, rows, :], sems.at[x])

    def body(x, carry):
        fs = [plane_at(all_ref, i, x) for i in range(19)]
        masks = [plane_at(mask_ref, p, x) for p in range(2)]
        wall = wall_terms([plane_at(vel_ref, k, x) for k in range(3)])
        f = arrive(
            fs,
            lambda i: plane_at(all_ref, i, x - DIRS[i][0]),
            lambda i: halo_ref[halo_slot(i), pl.ds(x - DIRS[i][0], 1), :],
            masks,
            wall,
        )
        for i in range(19):
            put_plane(made_ref, i, x, f[i])
        copy(x).start()
        return carry

    def finish(x, carry):
        copy(x).wait()
        return carry

    lax.fori_loop(1, CX - 1, body, 0)
    lax.fori_loop(1, CX - 1, finish, 0)


def edge_planes_kernel(
    fs_ref, halo_ref, mask_ref, vel_ref, inner_ref, outer_ref, mine_ref, whole_ref, out_ref, force_ref,
    made_ref, total_ref, sems,
):
    del whole_ref
    left_ref, right_ref = neighbours(inner_ref, outer_ref)
    total = mine_ref[...] + left_ref[5] + right_ref[5]
    for k in range(3):
        total_ref[k] = total[2 + k : 3 + k, 0:PER]
    copies = [pltpu.make_async_copy(total_ref, force_ref, sems.at[2])]
    copies[0].start()
    for side, (x, at_x, far_ref, far_dirs) in enumerate(((0, 0, left_ref, XP), (CX - 1, 3, right_ref, XM))):
        fs = [plane_at(fs_ref, i, at_x) for i in range(19)]
        masks = [plane_at(mask_ref, p, x) for p in range(2)]
        wall = wall_terms([plane_at(vel_ref, k, x) for k in range(3)])

        def source(i):
            if i in far_dirs:
                return far_ref[far_dirs.index(i)]
            return plane_at(fs_ref, i, at_x - DIRS[i][0])

        def halo_row(i):
            if i in far_dirs:
                n = 0 if DIRS[i][1] == 1 else 1
                return far_ref[5, n : n + 1, :]
            at = x - DIRS[i][0]
            return halo_ref[halo_slot(i), at : at + 1, :]

        f = arrive(fs, source, halo_row, masks, wall)
        for i in range(19):
            made_ref[side, i] = f[i]
        copy = pltpu.make_async_copy(made_ref.at[side], out_ref.at[:, pl.ds(x * CY, CY), :], sems.at[side])
        copy.start()
        copies.append(copy)
    for copy in copies:
        copy.wait()


def params(limit=VMEM_LIMIT):
    return pltpu.CompilerParams(vmem_limit_bytes=limit)


def cost(flops, nbytes):
    return pl.CostEstimate(flops=flops, bytes_accessed=nbytes, transcendentals=0)


def shape(*dims):
    return jax.ShapeDtypeStruct(dims, F32)


def shift(x, axis, by):
    count = lax.axis_size(axis)
    return lax.ppermute(x, axis, [(i, (i + by) % count) for i in range(count)])


def swap(x, axis, first):
    count = lax.axis_size(axis)
    pairs = [(i % count, (i + 1) % count) for i in range(first, first + count, 2)]
    return lax.ppermute(x, axis, pairs + [(b, a) for a, b in pairs])


def on_device(populations, link_mask, sphere_of_cell, sphere_velocity):
    pops = populations.reshape(19, ROWS, NZ)
    mask = link_mask.reshape(2, ROWS, NZ)
    ids = sphere_of_cell.reshape(ROWS, NZ)
    vel = jnp.transpose(sphere_velocity, (1, 0, 2))
    cells = ROWS * NZ
    xmsg = (6, CY, NZ)
    hbm = pl.BlockSpec(memory_space=pltpu.HBM)
    vmem = pl.BlockSpec(memory_space=pltpu.VMEM)

    to_inner, to_outer = pl.pallas_call(
        face_kernel,
        in_specs=[hbm, hbm],
        out_specs=[vmem, vmem],
        out_shape=[shape(*xmsg)] * 2,
        scratch_shapes=[
            pltpu.VMEM((2, 19, CY, NZ), F32),
            pltpu.VMEM((3, 1, PER), F32),
            pltpu.SemaphoreType.DMA((3,)),
        ],
        compiler_params=params(213 * 256 * 1024),
        name="faces",
    )(pops, vel)
    inner = swap(to_inner, "row", 0)
    outer = swap(to_outer, "row", 1)

    fs1 = pl.pallas_call(
        collide_kernel,
        out_shape=shape(19, ROWS, NZ),
        compiler_params=params(),
        cost_estimate=cost(300 * cells, 38 * 4 * cells),
        name="collide",
    )(pops)

    up, down = pl.pallas_call(
        row_kernel,
        out_shape=[shape(YMSG, NZ)] * 2,
        compiler_params=params(),
        name="y_rows",
    )(fs1, mask, ids, inner, outer, to_inner)
    below = shift(up, "col", 1)
    above = shift(down, "col", -1)

    f1, fs2, cell_vel, sums = pl.pallas_call(
        first_step_kernel,
        out_shape=[shape(19, ROWS, NZ), shape(19, ROWS, NZ), shape(3, ROWS, NZ), shape(16, NZ)],
        scratch_shapes=[
            pltpu.VMEM((2 * 18 * CY, CX * NZ), F32),
            pltpu.VMEM((LO * CY, CX * NZ), jnp.bfloat16),
        ],
        compiler_params=params(),
        cost_estimate=cost(1000 * cells, 70 * 4 * cells),
        name="first_step",
    )(fs1, mask, ids, inner, outer, to_inner)

    rows2, halo, to_inner2, to_outer2, mine = pl.pallas_call(
        second_step_kernel,
        out_shape=[shape(19, 2 * CX, NZ), shape(10, CX, NZ), shape(*xmsg), shape(*xmsg), shape(CY, NZ)],
        scratch_shapes=[
            pltpu.VMEM((2 * 18 * CY, 4 * NZ), F32),
            pltpu.VMEM((LO * CY, 4 * NZ), jnp.bfloat16),
        ],
        compiler_params=params(),
        name="second_step",
    )(fs1, f1, fs2, mask, ids, sums, inner, outer, below, above)
    inner2 = swap(to_inner2, "row", 0)
    outer2 = swap(to_outer2, "row", 1)

    whole, edges = pl.pallas_call(
        inner_planes_kernel,
        out_shape=[shape(19, ROWS, NZ), shape(19, 4 * CY, NZ)],
        out_specs=[hbm, vmem],
        scratch_shapes=[
            pltpu.VMEM((19, ROWS, NZ), F32),
            pltpu.VMEM((19, ROWS, NZ), F32),
            pltpu.SemaphoreType.DMA((CX,)),
        ],
        compiler_params=params(),
        cost_estimate=cost(300 * cells, 45 * 4 * cells),
        name="inner_planes",
    )(fs2, rows2, halo, mask, cell_vel)

    out, force = pl.pallas_call(
        edge_planes_kernel,
        in_specs=[vmem] * 7 + [hbm],
        out_specs=[hbm, hbm],
        out_shape=[shape(19, ROWS, NZ), shape(3, 1, PER)],
        scratch_shapes=[
            pltpu.VMEM((2, 19, CY, NZ), F32),
            pltpu.VMEM((3, 1, PER), F32),
            pltpu.SemaphoreType.DMA((3,)),
        ],
        input_output_aliases={7: 0},
        compiler_params=params(),
        name="edge_planes",
    )(edges, halo, mask, cell_vel, inner2, outer2, mine, whole)

    return out.reshape(19, CX, CY, NZ), jnp.transpose(force, (1, 0, 2))


def solution(mesh):
    in_specs = (
        P(None, "row", "col", None),
        P(None, "row", "col", None),
        P("row", "col", None),
        P("col", None, "row"),
    )
    out_specs = (P(None, "row", "col", None), P("col", None, "row"))
    return jax.shard_map(on_device, mesh=mesh, in_specs=in_specs, out_specs=out_specs, check_vma=False)
```

time: 59.9 us -> 55.8 us (0.932)
  starting transfers between devices: 35.6 us -> 32.6 us
  local copies, waits for them, and re-layouts: 2.55 us -> 0.79 us
  Pallas kernels: 8.5 us -> 9.46 us
    ppermute x6 -> x2, starting transfers between devices: 35.6 us -> 14.6 us  [shift(): return lax.ppermute(x, axis, [(i, (i + by) % count) for i in range(count)])]
    ppermute x0 -> x4, starting transfers between devices: none -> 18 us  [swap(): return lax.ppermute(x, axis, pairs + [(b, a) for a, b in pairs])]
    ppermute x6 -> x2, waiting for transfers between devices: 12 us -> 9.07 us  [shift(): return lax.ppermute(x, axis, [(i, (i + by) % count) for i in range(count)])]
    ppermute x0 -> x4, waiting for transfers between devices: none -> 2.76 us  [swap(): return lax.ppermute(x, axis, pairs + [(b, a) for a, b in pairs])]
    unnamed x8, local copies, waits for them, and re-layouts: 2.55 us -> 0.79 us
    pallas_call x5, Pallas kernels: 7.47 us -> 8.43 us  [the longest x1 3.64 us: on_device(): pl.pallas_call(first_step_kernel, out_shape=[shape(19, ROWS, NZ), shape(1...]
  transfers between devices with their start and end apart: 6 -> 6, of which waited for: 3 -> 4; matrix products, arithmetic and copies ran while one was open for 0% -> 0% of each run, Pallas kernels for 8% -> 12%
where the time goes in v2:
time: 55.8 us; the launch traced here: 55.4 us
  starting transfers between devices  32.6 us (58%)
  waiting for transfers between devices  11.8 us (21%)
  Pallas kernels  9.46 us (17%)
  local copies, waits for them, and re-layouts  0.79 us (1%)
  between operations  0.77 us (1%)
    ppermute x4, starting transfers between devices, swap(): return lax.ppermute(x, axis, pairs + [(b, a) for a, b in pairs])  18 us
    ppermute x2, starting transfers between devices, shift(): return lax.ppermute(x, axis, [(i, (i + by) % count) for i in range(count)])  14.6 us
    ppermute x2, waiting for transfers between devices, shift(): return lax.ppermute(x, axis, [(i, (i + by) % count) for i in range(count)])  9.07 us
    pallas_call x1, Pallas kernels, on_device(): pl.pallas_call(first_step_kernel, out_shape=[shape(19, ROWS, NZ), shape(1...  3.64 us
    ppermute x4, waiting for transfers between devices, swap(): return lax.ppermute(x, axis, pairs + [(b, a) for a, b in pairs])  2.76 us
    pallas_call x1, Pallas kernels, on_device(): pl.pallas_call(inner_planes_kernel, out_shape=[shape(19, ROWS, NZ), shape...  2.12 us
  transfers between devices with their start and end apart: 6, of which 4 were waited for; matrix products, arithmetic and copies ran while one was open for 0% of the time, Pallas kernels for 12%

profile of v2, /device:TPU:56, one launch (start us, length us, event | category | flops | bytes accessed | tf_op | source)
XLA Modules:
  0.0 55.4 jit_solution(7614315895137301256)
XLA Ops:
  0.6 0.0 copy-start
  0.6 0.0 copy-start.3
  0.6 0.8 %copy-done.3 = f32[1,3,64]{2,0,1:T(1,128)S(1)} copy-done((f32[1,3,64]{2,0,1:T(1,128)S(1)}, f32[1,3,64]{2,0,1:T(1,128)}, u32[]{:S(2)}) %copy-start.3) | copy-done | bytes 792
  1.4 1.0 %faces.1 = (f32[6,8,128]{2,1,0:T(8,128)S(1)}, f32[6,8,128]{2,1,0:T(8,128)S(1)}) custom-call(f32[19,128,128]{2,1,0:T(8,128)} %bitcast.6, f32[3,1,64]{2,1,0:T(1,128)S(1)} %bitcast.16), custom_call_target="tpu_custom_call" | custom-call | tf_op jit(solution)/shard_map/faces/pallas_call | solution.py:563
  2.4 9.5 %collective-permute-start.1 = (f32[6,8,128]{2,1,0:T(8,128)S(1)}, f32[6,8,128]{2,1,0:T(8,128)S(1)}, u32[]{:S(2)}, u32[]{:S(2)}) collective-permute-start(f32[6,8,128]{2,1,0:T(8,128)S(1)} %get-tuple-element.20), channel_id=1, source_target_pairs={{24,48},{72,96},{120,144},{168,192},{216,240},{264,288},{312,336},... | collective-permute-start | bytes 73736 | tf_op jit(solution)/shard_map/ppermute | solution.py:550
  12.0 0.0 copy-start.1
  12.0 0.0 copy-start.2
  12.0 2.1 %collective-permute-start = (f32[6,8,128]{2,1,0:T(8,128)S(1)}, f32[6,8,128]{2,1,0:T(8,128)S(1)}, u32[]{:S(2)}, u32[]{:S(2)}) collective-permute-start(f32[6,8,128]{2,1,0:T(8,128)S(1)} %get-tuple-element.19.own_ref), channel_id=1, source_target_pairs={{0,24},{48,72},{96,120},{144,168},{192,216},{240,264},{288,312},{3... | collective-permute-start | bytes 73736 | tf_op jit(solution)/shard_map/ppermute | solution.py:550
  14.0 0.0 copy-done
  14.1 0.8 %collide.1.fs_ref = f32[19,128,128]{2,1,0:T(8,128)S(1)} custom-call(f32[19,128,128]{2,1,0:T(8,128)S(1)} %bitcast.7), custom_call_target="tpu_custom_call" | custom-call | flops 4915200 | bytes 2490368 | tf_op jit(solution)/shard_map/collide/pallas_call | solution.py:579
  14.9 0.0 collective-permute-done.1.outer_ref
  14.9 0.3 collective-permute-done.inner_ref
  15.2 0.0 copy-done.1
  15.2 0.0 copy-done.2
  15.2 0.2 y_rows.1
  15.4 10.6 %collective-permute-start.2 = (f32[264,128]{1,0:T(8,128)S(1)}, f32[264,128]{1,0:T(8,128)S(1)}, u32[]{:S(2)}, u32[]{:S(2)}) collective-permute-start(f32[264,128]{1,0:T(8,128)S(1)} %get-tuple-element.24), channel_id=1, source_target_pairs={{0,1},{1,2},{2,3},{3,4},{4,5},{5,6},{6,7},{7,8},{8,9},{9,10},{10,1... | collective-permute-start | bytes 405512 | tf_op jit(solution)/shard_map/ppermute | solution.py:544
  26.1 3.9 %collective-permute-start.3 = (f32[264,128]{1,0:T(8,128)S(1)}, f32[264,128]{1,0:T(8,128)S(1)}, u32[]{:S(2)}, u32[]{:S(2)}) collective-permute-start(f32[264,128]{1,0:T(8,128)S(1)} %get-tuple-element.25), channel_id=1, source_target_pairs={{0,23},{1,0},{2,1},{3,2},{4,3},{5,4},{6,5},{7,6},{8,7},{9,8},{10,9... | collective-permute-start | bytes 405512 | tf_op jit(solution)/shard_map/ppermute | solution.py:544
  30.0 3.6 %first_step.1 = (f32[19,128,128]{2,1,0:T(8,128)S(1)}, f32[19,128,128]{2,1,0:T(8,128)S(1)}, f32[3,128,128]{2,1,0:T(8,128)S(1)}, f32[16,128]{1,0:T(8,128)S(1)}) custom-call(f32[19,128,128]{2,1,0:T(8,128)S(1)} %collide.1.fs_ref, s32[2,128,128]{2,1,0:T(8,128)S(1)} %bitcast.9, s32[128,128]{1,0:T(8,128)S(1)} %bitcast.14, ...), custom_call_target="tpu_custom_call" | custom-call | flops 16384000 | bytes 4587520 | tf_op jit(solution)/shard_map/first_step/pallas_call | solution.py:596
  33.7 3.6 %collective-permute-done.2.below_ref = f32[264,128]{1,0:T(8,128)S(1)} collective-permute-done((f32[264,128]{1,0:T(8,128)S(1)}, f32[264,128]{1,0:T(8,128)S(1)}, u32[]{:S(2)}, u32[]{:S(2)}) %collective-permute-start.2) | collective-permute-done | bytes 135200 | tf_op jit(solution)/shard_map/ppermute | solution.py:544
  37.3 5.5 %collective-permute-done.3.above_ref = f32[264,128]{1,0:T(8,128)S(1)} collective-permute-done((f32[264,128]{1,0:T(8,128)S(1)}, f32[264,128]{1,0:T(8,128)S(1)}, u32[]{:S(2)}, u32[]{:S(2)}) %collective-permute-start.3) | collective-permute-done | bytes 135200 | tf_op jit(solution)/shard_map/ppermute | solution.py:544
  42.7 0.9 %second_step.1 = (f32[19,32,128]{2,1,0:T(8,128)S(1)}, f32[10,16,128]{2,1,0:T(8,128)S(1)}, f32[6,8,128]{2,1,0:T(8,128)S(1)}, f32[6,8,128]{2,1,0:T(8,128)S(1)}, f32[8,128]{1,0:T(8,128)S(1)}) custom-call(f32[19,128,128]{2,1,0:T(8,128)S(1)} %collide.1.fs_ref, f32[19,128,128]{2,1,0:T(8,128)S(1)} %get-tuple-element.22.f_ref, ...), custom_call_target="tpu_custom_call" | custom-call | tf_op jit(solution)/shard_map/second_step/pallas_call | solution.py:608
  43.7 1.9 %collective-permute-start.4 = (f32[6,8,128]{2,1,0:T(8,128)S(1)}, f32[6,8,128]{2,1,0:T(8,128)S(1)}, u32[]{:S(2)}, u32[]{:S(2)}) collective-permute-start(f32[6,8,128]{2,1,0:T(8,128)S(1)} %get-tuple-element.30), channel_id=1, source_target_pairs={{0,24},{48,72},{96,120},{144,168},{192,216},{240,264},{288,312},{3... | collective-permute-start | bytes 73736 | tf_op jit(solution)/shard_map/ppermute | solution.py:550
  45.6 4.5 %collective-permute-start.5 = (f32[6,8,128]{2,1,0:T(8,128)S(1)}, f32[6,8,128]{2,1,0:T(8,128)S(1)}, u32[]{:S(2)}, u32[]{:S(2)}) collective-permute-start(f32[6,8,128]{2,1,0:T(8,128)S(1)} %get-tuple-element.31), channel_id=1, source_target_pairs={{24,48},{72,96},{120,144},{168,192},{216,240},{264,288},{312,336},... | collective-permute-start | bytes 73736 | tf_op jit(solution)/shard_map/ppermute | solution.py:550
  50.1 2.1 %inner_planes.1 = (f32[19,128,128]{2,1,0:T(8,128)}, f32[19,32,128]{2,1,0:T(8,128)S(1)}) custom-call(f32[19,128,128]{2,1,0:T(8,128)S(1)} %get-tuple-element.21.fs2_ref.fs_ref, f32[19,32,128]{2,1,0:T(8,128)S(1)} %get-tuple-element.26.row_ref, f32[10,16,128]{2,1,0:T(8,128)S(1)} %get-tuple-element.27.halo_ref, s32[2,128,128]{2,1,0:T(8,128)S(1)} %bitcast.11, ...), custom_call_target="tpu_custom_call" | custom-call | flops 4915200 | bytes 2949120 | tf_op jit(solution)/shard_map/inner_planes/pallas_call | solution.py:621
  52.2 0.0 collective-permute-done.4.inner_ref
  52.2 2.4 %collective-permute-done.5.outer_ref = f32[6,8,128]{2,1,0:T(8,128)S(1)} collective-permute-done((f32[6,8,128]{2,1,0:T(8,128)S(1)}, f32[6,8,128]{2,1,0:T(8,128)S(1)}, u32[]{:S(2)}, u32[]{:S(2)}) %collective-permute-start.5) | collective-permute-done | bytes 24608 | tf_op jit(solution)/shard_map/ppermute | solution.py:550
  54.6 0.8 %edge_planes.1 = (f32[19,128,128]{2,1,0:T(8,128)}, f32[3,1,64]{2,1,0:T(1,128)}) custom-call(f32[19,32,128]{2,1,0:T(8,128)S(1)} %get-tuple-element.29.fs_ref, f32[10,16,128]{2,1,0:T(8,128)S(1)} %get-tuple-element.27.halo_ref, s32[2,128,128]{2,1,0:T(8,128)S(1)} %bitcast.12, ...), custom_call_target="tpu_custom_call", output_to_operand_aliasing={{0}: (7, {})} | custom-call | tf_op jit(solution)/shard_map/edge_planes/pallas_call | solution.py:635
Async XLA Ops:
  0.6 13.4 %copy-start = (f32[19,16,8,128]{3,2,1,0:T(8,128)S(1)}, f32[19,16,8,128]{3,2,1,0:T(8,128)}, u32[]{:S(2)}) copy-start(f32[19,16,8,128]{3,2,1,0:T(8,128)} %param.4) | copy-start | bytes 3735556
  0.6 0.8 %copy-start.3 = (f32[1,3,64]{2,0,1:T(1,128)S(1)}, f32[1,3,64]{2,0,1:T(1,128)}, u32[]{:S(2)}) copy-start(f32[1,3,64]{2,0,1:T(1,128)} %param.7) | copy-start | bytes 2308
  2.4 12.4 %collective-permute-start.1 = (f32[6,8,128]{2,1,0:T(8,128)S(1)}, f32[6,8,128]{2,1,0:T(8,128)S(1)}, u32[]{:S(2)}, u32[]{:S(2)}) collective-permute-start(f32[6,8,128]{2,1,0:T(8,128)S(1)} %get-tuple-element.20), channel_id=1, source_target_pairs={{24,48},{72,96},{120,144},{168,192},{216,240},{264,288},{312,336},... | collective-permute-start | bytes 73736 | tf_op jit(solution)/shard_map/ppermute | solution.py:550
  12.0 3.2 %copy-start.1 = (s32[2,16,8,128]{3,2,1,0:T(8,128)S(1)}, s32[2,16,8,128]{3,2,1,0:T(8,128)}, u32[]{:S(2)}) copy-start(s32[2,16,8,128]{3,2,1,0:T(8,128)} %param.5) | copy-start | bytes 393220
  12.0 3.2 %copy-start.2 = (s32[16,8,128]{2,1,0:T(8,128)S(1)}, s32[16,8,128]{2,1,0:T(8,128)}, u32[]{:S(2)}) copy-start(s32[16,8,128]{2,1,0:T(8,128)} %param.6) | copy-start | bytes 196612
  12.0 3.2 %collective-permute-start = (f32[6,8,128]{2,1,0:T(8,128)S(1)}, f32[6,8,128]{2,1,0:T(8,128)S(1)}, u32[]{:S(2)}, u32[]{:S(2)}) collective-permute-start(f32[6,8,128]{2,1,0:T(8,128)S(1)} %get-tuple-element.19.own_ref), channel_id=1, source_target_pairs={{0,24},{48,72},{96,120},{144,168},{192,216},{240,264},{288,312},{3... | collective-permute-start | bytes 73736 | tf_op jit(solution)/shard_map/ppermute | solution.py:550
  15.4 21.8 %collective-permute-start.2 = (f32[264,128]{1,0:T(8,128)S(1)}, f32[264,128]{1,0:T(8,128)S(1)}, u32[]{:S(2)}, u32[]{:S(2)}) collective-permute-start(f32[264,128]{1,0:T(8,128)S(1)} %get-tuple-element.24), channel_id=1, source_target_pairs={{0,1},{1,2},{2,3},{3,4},{4,5},{5,6},{6,7},{7,8},{8,9},{9,10},{10,1... | collective-permute-start | bytes 405512 | tf_op jit(solution)/shard_map/ppermute | solution.py:544
  26.1 16.7 %collective-permute-start.3 = (f32[264,128]{1,0:T(8,128)S(1)}, f32[264,128]{1,0:T(8,128)S(1)}, u32[]{:S(2)}, u32[]{:S(2)}) collective-permute-start(f32[264,128]{1,0:T(8,128)S(1)} %get-tuple-element.25), channel_id=1, source_target_pairs={{0,23},{1,0},{2,1},{3,2},{4,3},{5,4},{6,5},{7,6},{8,7},{9,8},{10,9... | collective-permute-start | bytes 405512 | tf_op jit(solution)/shard_map/ppermute | solution.py:544
  43.7 8.6 %collective-permute-start.4 = (f32[6,8,128]{2,1,0:T(8,128)S(1)}, f32[6,8,128]{2,1,0:T(8,128)S(1)}, u32[]{:S(2)}, u32[]{:S(2)}) collective-permute-start(f32[6,8,128]{2,1,0:T(8,128)S(1)} %get-tuple-element.30), channel_id=1, source_target_pairs={{0,24},{48,72},{96,120},{144,168},{192,216},{240,264},{288,312},{3... | collective-permute-start | bytes 73736 | tf_op jit(solution)/shard_map/ppermute | solution.py:550
  45.6 9.1 %collective-permute-start.5 = (f32[6,8,128]{2,1,0:T(8,128)S(1)}, f32[6,8,128]{2,1,0:T(8,128)S(1)}, u32[]{:S(2)}, u32[]{:S(2)}) collective-permute-start(f32[6,8,128]{2,1,0:T(8,128)S(1)} %get-tuple-element.31), channel_id=1, source_target_pairs={{24,48},{72,96},{120,144},{168,192},{216,240},{264,288},{312,336},... | collective-permute-start | bytes 73736 | tf_op jit(solution)/shard_map/ppermute | solution.py:550

commit v3 on v2

--- a/solution.py
+++ b/solution.py
@@ -490,7 +490,7 @@
 
 
 def edge_planes_kernel(
-    fs_ref, halo_ref, mask_ref, vel_ref, inner_ref, outer_ref, mine_ref, whole_ref, out_ref, force_ref,
+    fs_ref, halo_ref, mask_ref, vel_ref, outer_ref, inner_ref, mine_ref, whole_ref, out_ref, force_ref,
     made_ref, total_ref, sems,
 ):
     del whole_ref
@@ -555,6 +555,7 @@
     mask = link_mask.reshape(2, ROWS, NZ)
     ids = sphere_of_cell.reshape(ROWS, NZ)
     vel = jnp.transpose(sphere_velocity, (1, 0, 2))
+    vel = pltpu.with_memory_space_constraint(vel, pltpu.HBM)
     cells = ROWS * NZ
     xmsg = (6, CY, NZ)
     hbm = pl.BlockSpec(memory_space=pltpu.HBM)
@@ -645,7 +646,7 @@
         input_output_aliases={7: 0},
         compiler_params=params(),
         name="edge_planes",
-    )(edges, halo, mask, cell_vel, inner2, outer2, mine, whole)
+    )(edges, halo, mask, cell_vel, outer2, inner2, mine, whole)
 
     return out.reshape(19, CX, CY, NZ), jnp.transpose(force, (1, 0, 2))
 

time: 55.8 us -> 53.6 us (0.961)
  waiting for transfers between devices: 11.8 us -> 9.91 us
  local copies, waits for them, and re-layouts: 0.79 us -> 0.02 us
    ppermute x4, waiting for transfers between devices: 2.76 us -> 0.84 us  [swap(): return lax.ppermute(x, axis, pairs + [(b, a) for a, b in pairs])]
    unnamed x8 -> x6, local copies, waits for them, and re-layouts: 0.79 us -> 0.02 us
where the time goes in v3:
time: 53.6 us; the launch traced here: 52.8 us
  starting transfers between devices  32.6 us (61%)
  waiting for transfers between devices  9.91 us (18%)
  Pallas kernels  9.56 us (18%)
  between operations  0.76 us (1%)
    ppermute x4, starting transfers between devices, swap(): return lax.ppermute(x, axis, pairs + [(b, a) for a, b in pairs])  18 us
    ppermute x2, starting transfers between devices, shift(): return lax.ppermute(x, axis, [(i, (i + by) % count) for i in range(count)])  14.6 us
    ppermute x2, waiting for transfers between devices, shift(): return lax.ppermute(x, axis, [(i, (i + by) % count) for i in range(count)])  9.07 us
    pallas_call x1, Pallas kernels, on_device(): pl.pallas_call(first_step_kernel, out_shape=[shape(19, ROWS, NZ), shape(1...  3.65 us
    pallas_call x1, Pallas kernels, on_device(): pl.pallas_call(inner_planes_kernel, out_shape=[shape(19, ROWS, NZ), shape...  2.12 us
    pallas_call x1, Pallas kernels, on_device(): pl.pallas_call(face_kernel, in_specs=[hbm, hbm], out_specs=[vmem, vmem],...  1.09 us
  transfers between devices with their start and end apart: 6, of which 4 were waited for; matrix products, arithmetic and copies ran while one was open for 0% of the time, Pallas kernels for 12%

profile of v3, /device:TPU:56, one launch (start us, length us, event | category | flops | bytes accessed | tf_op | source)
XLA Modules:
  0.0 52.8 jit_solution(8790899924724268408)
XLA Ops:
  0.6 0.0 copy-start
  0.6 1.1 %faces.1 = (f32[6,8,128]{2,1,0:T(8,128)S(1)}, f32[6,8,128]{2,1,0:T(8,128)S(1)}) custom-call(f32[19,128,128]{2,1,0:T(8,128)} %bitcast.6, f32[3,1,64]{2,1,0:T(1,128)} %bitcast.17), custom_call_target="tpu_custom_call" | custom-call | tf_op jit(solution)/shard_map/faces/pallas_call | solution.py:564
  1.7 9.5 %collective-permute-start.1 = (f32[6,8,128]{2,1,0:T(8,128)S(1)}, f32[6,8,128]{2,1,0:T(8,128)S(1)}, u32[]{:S(2)}, u32[]{:S(2)}) collective-permute-start(f32[6,8,128]{2,1,0:T(8,128)S(1)} %get-tuple-element.20), channel_id=1, source_target_pairs={{24,48},{72,96},{120,144},{168,192},{216,240},{264,288},{312,336},... | collective-permute-start | bytes 73736 | tf_op jit(solution)/shard_map/ppermute | solution.py:550
  11.3 0.0 copy-start.1
  11.3 0.0 copy-start.2
  11.3 2.1 %collective-permute-start = (f32[6,8,128]{2,1,0:T(8,128)S(1)}, f32[6,8,128]{2,1,0:T(8,128)S(1)}, u32[]{:S(2)}, u32[]{:S(2)}) collective-permute-start(f32[6,8,128]{2,1,0:T(8,128)S(1)} %get-tuple-element.19.own_ref), channel_id=1, source_target_pairs={{0,24},{48,72},{96,120},{144,168},{192,216},{240,264},{288,312},{3... | collective-permute-start | bytes 73736 | tf_op jit(solution)/shard_map/ppermute | solution.py:550
  13.4 0.0 copy-done
  13.4 0.8 %collide.1.fs_ref = f32[19,128,128]{2,1,0:T(8,128)S(1)} custom-call(f32[19,128,128]{2,1,0:T(8,128)S(1)} %bitcast.7), custom_call_target="tpu_custom_call" | custom-call | flops 4915200 | bytes 2490368 | tf_op jit(solution)/shard_map/collide/pallas_call | solution.py:580
  14.2 0.0 collective-permute-done.1.outer_ref
  14.2 0.3 collective-permute-done.inner_ref
  14.5 0.0 copy-done.1
  14.5 0.0 copy-done.2
  14.5 0.2 y_rows.1
  14.8 10.6 %collective-permute-start.2 = (f32[264,128]{1,0:T(8,128)S(1)}, f32[264,128]{1,0:T(8,128)S(1)}, u32[]{:S(2)}, u32[]{:S(2)}) collective-permute-start(f32[264,128]{1,0:T(8,128)S(1)} %get-tuple-element.24), channel_id=1, source_target_pairs={{0,1},{1,2},{2,3},{3,4},{4,5},{5,6},{6,7},{7,8},{8,9},{9,10},{10,1... | collective-permute-start | bytes 405512 | tf_op jit(solution)/shard_map/ppermute | solution.py:544
  25.4 3.9 %collective-permute-start.3 = (f32[264,128]{1,0:T(8,128)S(1)}, f32[264,128]{1,0:T(8,128)S(1)}, u32[]{:S(2)}, u32[]{:S(2)}) collective-permute-start(f32[264,128]{1,0:T(8,128)S(1)} %get-tuple-element.25), channel_id=1, source_target_pairs={{0,23},{1,0},{2,1},{3,2},{4,3},{5,4},{6,5},{7,6},{8,7},{9,8},{10,9... | collective-permute-start | bytes 405512 | tf_op jit(solution)/shard_map/ppermute | solution.py:544
  29.3 3.7 %first_step.1 = (f32[19,128,128]{2,1,0:T(8,128)S(1)}, f32[19,128,128]{2,1,0:T(8,128)S(1)}, f32[3,128,128]{2,1,0:T(8,128)S(1)}, f32[16,128]{1,0:T(8,128)S(1)}) custom-call(f32[19,128,128]{2,1,0:T(8,128)S(1)} %collide.1.fs_ref, s32[2,128,128]{2,1,0:T(8,128)S(1)} %bitcast.9, s32[128,128]{1,0:T(8,128)S(1)} %bitcast.14, ...), custom_call_target="tpu_custom_call" | custom-call | flops 16384000 | bytes 4587520 | tf_op jit(solution)/shard_map/first_step/pallas_call | solution.py:597
  33.0 3.6 %collective-permute-done.2.below_ref = f32[264,128]{1,0:T(8,128)S(1)} collective-permute-done((f32[264,128]{1,0:T(8,128)S(1)}, f32[264,128]{1,0:T(8,128)S(1)}, u32[]{:S(2)}, u32[]{:S(2)}) %collective-permute-start.2) | collective-permute-done | bytes 135200 | tf_op jit(solution)/shard_map/ppermute | solution.py:544
  36.6 5.5 %collective-permute-done.3.above_ref = f32[264,128]{1,0:T(8,128)S(1)} collective-permute-done((f32[264,128]{1,0:T(8,128)S(1)}, f32[264,128]{1,0:T(8,128)S(1)}, u32[]{:S(2)}, u32[]{:S(2)}) %collective-permute-start.3) | collective-permute-done | bytes 135200 | tf_op jit(solution)/shard_map/ppermute | solution.py:544
  42.1 0.9 %second_step.1 = (f32[19,32,128]{2,1,0:T(8,128)S(1)}, f32[10,16,128]{2,1,0:T(8,128)S(1)}, f32[6,8,128]{2,1,0:T(8,128)S(1)}, f32[6,8,128]{2,1,0:T(8,128)S(1)}, f32[8,128]{1,0:T(8,128)S(1)}) custom-call(f32[19,128,128]{2,1,0:T(8,128)S(1)} %collide.1.fs_ref, f32[19,128,128]{2,1,0:T(8,128)S(1)} %get-tuple-element.22.f_ref, ...), custom_call_target="tpu_custom_call" | custom-call | tf_op jit(solution)/shard_map/second_step/pallas_call | solution.py:609
  43.0 4.5 %collective-permute-start.4 = (f32[6,8,128]{2,1,0:T(8,128)S(1)}, f32[6,8,128]{2,1,0:T(8,128)S(1)}, u32[]{:S(2)}, u32[]{:S(2)}) collective-permute-start(f32[6,8,128]{2,1,0:T(8,128)S(1)} %get-tuple-element.30), channel_id=1, source_target_pairs={{24,48},{72,96},{120,144},{168,192},{216,240},{264,288},{312,336},... | collective-permute-start | bytes 73736 | tf_op jit(solution)/shard_map/ppermute | solution.py:550
  47.5 1.9 %collective-permute-start.5 = (f32[6,8,128]{2,1,0:T(8,128)S(1)}, f32[6,8,128]{2,1,0:T(8,128)S(1)}, u32[]{:S(2)}, u32[]{:S(2)}) collective-permute-start(f32[6,8,128]{2,1,0:T(8,128)S(1)} %get-tuple-element.31), channel_id=1, source_target_pairs={{0,24},{48,72},{96,120},{144,168},{192,216},{240,264},{288,312},{3... | collective-permute-start | bytes 73736 | tf_op jit(solution)/shard_map/ppermute | solution.py:550
  49.4 2.1 %inner_planes.1 = (f32[19,128,128]{2,1,0:T(8,128)}, f32[19,32,128]{2,1,0:T(8,128)S(1)}) custom-call(f32[19,128,128]{2,1,0:T(8,128)S(1)} %get-tuple-element.21.fs2_ref.fs_ref, f32[19,32,128]{2,1,0:T(8,128)S(1)} %get-tuple-element.26.row_ref, f32[10,16,128]{2,1,0:T(8,128)S(1)} %get-tuple-element.27.halo_ref, s32[2,128,128]{2,1,0:T(8,128)S(1)} %bitcast.11, ...), custom_call_target="tpu_custom_call" | custom-call | flops 4915200 | bytes 2949120 | tf_op jit(solution)/shard_map/inner_planes/pallas_call | solution.py:622
  51.5 0.5 collective-permute-done.4.outer_ref
  52.0 0.0 collective-permute-done.5.inner_ref
  52.0 0.8 %edge_planes.1 = (f32[19,128,128]{2,1,0:T(8,128)}, f32[3,1,64]{2,1,0:T(1,128)}) custom-call(f32[19,32,128]{2,1,0:T(8,128)S(1)} %get-tuple-element.29.fs_ref, f32[10,16,128]{2,1,0:T(8,128)S(1)} %get-tuple-element.27.halo_ref, s32[2,128,128]{2,1,0:T(8,128)S(1)} %bitcast.12, ...), custom_call_target="tpu_custom_call", output_to_operand_aliasing={{0}: (7, {})} | custom-call | tf_op jit(solution)/shard_map/edge_planes/pallas_call | solution.py:636
Async XLA Ops:
  0.6 12.7 %copy-start = (f32[19,16,8,128]{3,2,1,0:T(8,128)S(1)}, f32[19,16,8,128]{3,2,1,0:T(8,128)}, u32[]{:S(2)}) copy-start(f32[19,16,8,128]{3,2,1,0:T(8,128)} %param.4) | copy-start | bytes 3735556
  1.7 12.4 %collective-permute-start.1 = (f32[6,8,128]{2,1,0:T(8,128)S(1)}, f32[6,8,128]{2,1,0:T(8,128)S(1)}, u32[]{:S(2)}, u32[]{:S(2)}) collective-permute-start(f32[6,8,128]{2,1,0:T(8,128)S(1)} %get-tuple-element.20), channel_id=1, source_target_pairs={{24,48},{72,96},{120,144},{168,192},{216,240},{264,288},{312,336},... | collective-permute-start | bytes 73736 | tf_op jit(solution)/shard_map/ppermute | solution.py:550
  11.3 3.2 %copy-start.1 = (s32[2,16,8,128]{3,2,1,0:T(8,128)S(1)}, s32[2,16,8,128]{3,2,1,0:T(8,128)}, u32[]{:S(2)}) copy-start(s32[2,16,8,128]{3,2,1,0:T(8,128)} %param.5) | copy-start | bytes 393220
  11.3 3.2 %copy-start.2 = (s32[16,8,128]{2,1,0:T(8,128)S(1)}, s32[16,8,128]{2,1,0:T(8,128)}, u32[]{:S(2)}) copy-start(s32[16,8,128]{2,1,0:T(8,128)} %param.6) | copy-start | bytes 196612
  11.3 3.2 %collective-permute-start = (f32[6,8,128]{2,1,0:T(8,128)S(1)}, f32[6,8,128]{2,1,0:T(8,128)S(1)}, u32[]{:S(2)}, u32[]{:S(2)}) collective-permute-start(f32[6,8,128]{2,1,0:T(8,128)S(1)} %get-tuple-element.19.own_ref), channel_id=1, source_target_pairs={{0,24},{48,72},{96,120},{144,168},{192,216},{240,264},{288,312},{3... | collective-permute-start | bytes 73736 | tf_op jit(solution)/shard_map/ppermute | solution.py:550
  14.8 21.8 %collective-permute-start.2 = (f32[264,128]{1,0:T(8,128)S(1)}, f32[264,128]{1,0:T(8,128)S(1)}, u32[]{:S(2)}, u32[]{:S(2)}) collective-permute-start(f32[264,128]{1,0:T(8,128)S(1)} %get-tuple-element.24), channel_id=1, source_target_pairs={{0,1},{1,2},{2,3},{3,4},{4,5},{5,6},{6,7},{7,8},{8,9},{9,10},{10,1... | collective-permute-start | bytes 405512 | tf_op jit(solution)/shard_map/ppermute | solution.py:544
  25.4 16.7 %collective-permute-start.3 = (f32[264,128]{1,0:T(8,128)S(1)}, f32[264,128]{1,0:T(8,128)S(1)}, u32[]{:S(2)}, u32[]{:S(2)}) collective-permute-start(f32[264,128]{1,0:T(8,128)S(1)} %get-tuple-element.25), channel_id=1, source_target_pairs={{0,23},{1,0},{2,1},{3,2},{4,3},{5,4},{6,5},{7,6},{8,7},{9,8},{10,9... | collective-permute-start | bytes 405512 | tf_op jit(solution)/shard_map/ppermute | solution.py:544
  43.0 9.1 %collective-permute-start.4 = (f32[6,8,128]{2,1,0:T(8,128)S(1)}, f32[6,8,128]{2,1,0:T(8,128)S(1)}, u32[]{:S(2)}, u32[]{:S(2)}) collective-permute-start(f32[6,8,128]{2,1,0:T(8,128)S(1)} %get-tuple-element.30), channel_id=1, source_target_pairs={{24,48},{72,96},{120,144},{168,192},{216,240},{264,288},{312,336},... | collective-permute-start | bytes 73736 | tf_op jit(solution)/shard_map/ppermute | solution.py:550
  47.5 4.6 %collective-permute-start.5 = (f32[6,8,128]{2,1,0:T(8,128)S(1)}, f32[6,8,128]{2,1,0:T(8,128)S(1)}, u32[]{:S(2)}, u32[]{:S(2)}) collective-permute-start(f32[6,8,128]{2,1,0:T(8,128)S(1)} %get-tuple-element.31), channel_id=1, source_target_pairs={{0,24},{48,72},{96,120},{144,168},{192,216},{240,264},{288,312},{3... | collective-permute-start | bytes 73736 | tf_op jit(solution)/shard_map/ppermute | solution.py:550
